TPU v7x, 32 devices: a whole 2x2x4 slice. The times are simulated.
32 devices in a mesh: phase: 2 (over x), seq: 16 (over z, y, core).
Axes of the slice: x: 2, y: 2, z: 4, core: 2. Of those that a mesh axis runs over, the one named last changes fastest.
Arguments:
- dec_in: bfloat16 [2, 512, 4096], P(None, None, 'seq'), may hold values from -6 to 6
- enc_kv: bfloat16 [2, 2, 2048, 8192], P('phase', None, 'seq'), may hold values from -15 to 15
- dec_seg: int32 [2, 512], replicated, may hold values from 0 to 3, never falling along the last dimension, each value on 1 to 256 neighbouring positions
- enc_seg: int32 [2, 2048], replicated, may hold values from 0 to 3, never falling along the last dimension, each value on 1 to 1024 neighbouring positions
- q_gain: float32 [2, 4096], P('phase', 'seq'), may hold values from 0.5 to 1.5
- o_gain: float32 [2, 4096], P('phase', 'seq'), may hold values from 1 to 8
- cotangent: bfloat16 [2, 512, 4096], P(None, None, 'seq'), may hold values from -6 to 6
Outputs:
- sect_out: bfloat16 [2, 2, 512, 4096], P('phase', None, None, 'seq')
- grad_kv: bfloat16 [2, 2, 2048, 8192], P('phase', None, 'seq')
- grad_q_gain: float32 [2, 4096], P('phase', 'seq')
- grad_o_gain: float32 [2, 4096], P('phase', 'seq')
Inputs may be any that keep to these rules, and one draw needn't show every extreme that they name: `dec_seg`: every one of the 4 documents has positions in both the decoder and the encoder of each micro-batch.
All inputs are finite; a program needn't handle non-finite values.
Results may differ from a plain program's by a relative error of at most 0.0075.
The roundings to bfloat16 on the way count: a program that leaves them out, or rounds other values in their place, can miss the bound.
Values may be sent and summed in bfloat16 or wider, within the bound.
A program may use at most 192 MiB of HBM per device.

v0:
```python
import math

import jax
import jax.numpy as jnp
from jax import lax
from jax.sharding import PartitionSpec as P

D = 4096
HEAD = 64
QROWS = 256


eps = 1e-06
neg_big = -1e30


def from_behind(value, axis, steps):
    count = lax.axis_size(axis)
    first, last = (max(0, -steps), min(count, count - steps))
    return lax.ppermute(value, axis, [(source, source + steps) for source in range(first, last)])


def attend(query, keyval, qseg, kseg):
    scale = 1.0 / math.sqrt(HEAD)
    keys = keyval[:, :, 0, :]
    values = keyval[:, :, 1, :]
    scores = jnp.einsum("rhd,ehd->hre", query, keys, preferred_element_type=jnp.float32) * scale
    allowed = qseg[:, None] == kseg[None, :]
    scores = jnp.where(allowed[None, :, :], scores, neg_big)
    top = jnp.max(scores, axis=2, keepdims=True)
    expo = jnp.exp(scores - top)
    probs = expo / jnp.sum(expo, axis=2, keepdims=True)
    weights = probs.astype(jnp.bfloat16)
    output = jnp.einsum("hre,ehd->rhd", weights, values, preferred_element_type=jnp.float32)
    return (output, probs, weights)


def attend_rows(query, keyval, qseg, kseg):
    blocks = query.shape[0] // QROWS
    query_blocks = query.reshape(blocks, QROWS, query.shape[1], query.shape[2])
    seg_blocks = qseg.reshape(blocks, QROWS)

    def one_block(item):
        return attend(item[0], keyval, item[1], kseg)[0]

    output = lax.map(one_block, (query_blocks, seg_blocks))
    return output.reshape(query.shape)


def attend_rows_back(query, keyval, qseg, kseg, grad_out):
    scale = 1.0 / math.sqrt(HEAD)
    keys = keyval[:, :, 0, :]
    values = keyval[:, :, 1, :]
    blocks = query.shape[0] // QROWS
    query_blocks = query.reshape(blocks, QROWS, query.shape[1], query.shape[2])
    grad_blocks = grad_out.reshape(blocks, QROWS, query.shape[1], query.shape[2])
    seg_blocks = qseg.reshape(blocks, QROWS)

    def one_block(summed, item):
        qblock, sblock, gblock = item
        output, probs, weights = attend(qblock, keyval, sblock, kseg)
        grad_low = gblock.astype(jnp.bfloat16)
        grad_values = jnp.einsum(
            "hre,rhd->ehd", weights, grad_low, preferred_element_type=jnp.float32
        )
        grad_probs = jnp.einsum(
            "rhd,ehd->hre", grad_low, values, preferred_element_type=jnp.float32
        )
        delta = jnp.sum(probs * grad_probs, axis=2, keepdims=True)
        grad_scores = (probs * (grad_probs - delta) * scale).astype(jnp.bfloat16)
        grad_query = jnp.einsum(
            "hre,ehd->rhd", grad_scores, keys, preferred_element_type=jnp.float32
        )
        grad_keys = jnp.einsum(
            "hre,rhd->ehd", grad_scores, qblock, preferred_element_type=jnp.float32
        )
        return (summed + jnp.stack([grad_keys, grad_values], axis=2), (grad_query, output))

    start = jnp.zeros((keyval.shape[0], keyval.shape[1], 2, HEAD), jnp.float32)
    summed, outputs = lax.scan(one_block, start, (query_blocks, seg_blocks, grad_blocks))
    return (summed, outputs[0].reshape(query.shape), outputs[1].reshape(query.shape))


def prepare(xf, total, qgain):
    inv = lax.rsqrt(total / D + eps)
    normed = xf * inv[:, None]
    query = (normed * qgain[None, :]).astype(jnp.bfloat16)
    return (inv, normed, query.reshape(xf.shape[0], xf.shape[1] // HEAD, HEAD))


def section_forward(x, keyval_flat, qseg, kseg, qgain, ogain):
    xf = x.astype(jnp.float32)
    total = lax.psum(jnp.sum(xf * xf, axis=1), "seq")
    inv, normed, query = prepare(xf, total, qgain)
    keyval = keyval_flat.reshape(keyval_flat.shape[0], x.shape[1] // HEAD, 2, HEAD)
    output = attend_rows(query, keyval, qseg, kseg).reshape(x.shape)
    return ((xf + ogain[None, :] * output).astype(jnp.bfloat16), total)


def section_backward(x, total, keyval_flat, qseg, kseg, qgain, ogain, grad_y):
    xf = x.astype(jnp.float32)
    inv, normed, query = prepare(xf, total, qgain)
    keyval = keyval_flat.reshape(keyval_flat.shape[0], x.shape[1] // HEAD, 2, HEAD)
    grad_f = grad_y.astype(jnp.float32)
    grad_out = (grad_f * ogain[None, :]).reshape(query.shape)
    summed, grad_query, output = attend_rows_back(query, keyval, qseg, kseg, grad_out)
    grad_query = grad_query.reshape(x.shape)
    output = output.reshape(x.shape)
    grad_pair = summed.reshape(summed.shape[0], 2 * x.shape[1]).astype(jnp.bfloat16)
    grad_qg = jnp.sum(grad_query * normed, axis=0)
    grad_og = jnp.sum(grad_f * output, axis=0)
    grad_normed = grad_query * qgain[None, :]
    cross = lax.psum(jnp.sum(grad_normed * xf, axis=1), "seq")
    grad_x = (
        grad_f + inv[:, None] * grad_normed - xf * (inv * inv * inv)[:, None] * (cross / D)[:, None]
    )
    return (grad_x.astype(jnp.bfloat16), grad_pair, grad_qg, grad_og)


def local(dec_in, enc_kv, dec_seg, enc_seg, q_gain, o_gain, cotangent):
    phase = lax.axis_index("phase")
    micro = dec_in.shape[0]
    rows = dec_in.shape[1]
    feats = dec_in.shape[2]
    local_kv = enc_kv[0]
    qgain = q_gain[0]
    ogain = o_gain[0]
    enc_rows = enc_seg.shape[1]
    kv_buf = lax.all_to_all(local_kv, "seq", split_axis=2, concat_axis=1, tiled=True)
    carried = jnp.zeros((rows, feats), jnp.bfloat16)
    inputs = []
    totals = []
    outputs = []
    for step in range(micro + 1):
        offset = step - phase
        index = jnp.clip(offset, 0, micro - 1)
        live = (offset >= 0) & (offset < micro)
        x = jnp.where(phase == 0, dec_in[min(step, micro - 1)], carried)
        kv_now = lax.dynamic_index_in_dim(kv_buf, index, 0, keepdims=False)
        qseg = lax.dynamic_index_in_dim(dec_seg, index, 0, keepdims=False)
        kseg = lax.dynamic_index_in_dim(enc_seg, index, 0, keepdims=False)
        result, total = section_forward(x, kv_now, qseg, kseg, qgain, ogain)
        inputs.append(x)
        totals.append(total)
        outputs.append(result)
        if step < micro:
            carried = from_behind(result, "phase", 1)
    sect_out = jnp.stack([jnp.where(phase == 0, outputs[m], outputs[m + 1]) for m in range(micro)])
    stacked_inputs = jnp.stack(inputs)
    stacked_totals = jnp.stack(totals)
    grad_carried = jnp.zeros((rows, feats), jnp.bfloat16)
    grad_buf = jnp.zeros((micro, enc_rows, 2 * feats), jnp.bfloat16)
    qg_sum = jnp.zeros((feats,), jnp.float32)
    og_sum = jnp.zeros((feats,), jnp.float32)
    for back in range(micro + 1):
        offset = back - 1 + phase
        index = jnp.clip(offset, 0, micro - 1)
        live = (offset >= 0) & (offset < micro)
        fwd_step = jnp.clip(index + phase, 0, micro)
        x = lax.dynamic_index_in_dim(stacked_inputs, fwd_step, 0, keepdims=False)
        total = lax.dynamic_index_in_dim(stacked_totals, fwd_step, 0, keepdims=False)
        grad_y = jnp.where(phase == 1, cotangent[min(back, micro - 1)], grad_carried)
        kv_now = lax.dynamic_index_in_dim(kv_buf, index, 0, keepdims=False)
        qseg = lax.dynamic_index_in_dim(dec_seg, index, 0, keepdims=False)
        kseg = lax.dynamic_index_in_dim(enc_seg, index, 0, keepdims=False)
        grad_x, grad_pair, grad_qg, grad_og = section_backward(
            x, total, kv_now, qseg, kseg, qgain, ogain, grad_y
        )
        grad_buf = jnp.where(
            live, lax.dynamic_update_index_in_dim(grad_buf, grad_pair, index, 0), grad_buf
        )
        qg_sum = qg_sum + jnp.where(live, grad_qg, 0.0)
        og_sum = og_sum + jnp.where(live, grad_og, 0.0)
        if back < micro:
            grad_carried = from_behind(grad_x, "phase", -1)
    grad_rows = lax.all_to_all(grad_buf, "seq", split_axis=1, concat_axis=2, tiled=True)
    return (sect_out[None], grad_rows[None], qg_sum[None], og_sum[None])


def solution(mesh):
    in_specs = (
        P(None, None, "seq"),
        P("phase", None, "seq", None),
        P(),
        P(),
        P("phase", "seq"),
        P("phase", "seq"),
        P(None, None, "seq"),
    )
    out_specs = (
        P("phase", None, None, "seq"),
        P("phase", None, "seq", None),
        P("phase", "seq"),
        P("phase", "seq"),
    )
    return jax.shard_map(local, mesh=mesh, in_specs=in_specs, out_specs=out_specs, check_vma=False)
```

profile of v0, /device:TPU:13, one launch (start us, length us, event | category | flops | bytes accessed | tf_op | source)
XLA Modules:
  0.0 1053.2 jit_solution(4034067064642536242)
XLA Ops:
  19.3 108.3 %psum.35 = f32[512]{0:T(512)S(1)} all-reduce(f32[512]{0:T(512)S(1)} %get-tuple-element.720), channel_id=1, replica_groups=mesh['phase'=2,'seq'=16] {'seq'}, use_global_device_ids=true, to_apply=%region_1.2 | all-reduce | flops 512 | bytes 4096 | tf_op jit(solution)/shard_map/psum | solution.py:93
  160.2 32.8 %while.75 = (s32[]{:T(128)}, f32[2,256,4,64]{1,0,3,2:T(2,128)S(1)}, s32[2,256]{1,0:T(2,128)S(1)}, s32[2048]{0:T(1024)S(1)}, bf16[2,256,4,64]{1,3,2,0:T(8,128)(2,...) while((s32[]{:T(128)}, f32[2,256,4,64]{1,0,3,2:T(2,128)S(1)}, ...), condition=%wide.region_5.6_spmd, body=%wide.region_2.5_spmd.sunk | while | flops 554174464 | bytes 38161504 | solution.py:46
  220.9 22.6 %psum.36 = f32[512]{0:T(512)S(1)} all-reduce(f32[512]{0:T(512)S(1)} %get-tuple-element.718), channel_id=1, replica_groups=mesh['phase'=2,'seq'=16] {'seq'}, use_global_device_ids=true, to_apply=%region_7.8 | all-reduce | flops 512 | bytes 4096 | tf_op jit(solution)/shard_map/psum | solution.py:93
  243.9 35.7 %while.76 = (s32[]{:T(128)}, f32[2,256,4,64]{1,0,3,2:T(2,128)S(1)}, s32[2,256]{1,0:T(2,128)S(1)}, s32[2048]{0:T(1024)S(1)}, bf16[2,256,4,64]{1,3,2,0:T(8,128)(2,...) while((s32[]{:T(128)}, f32[2,256,4,64]{1,0,3,2:T(2,128)S(1)}, s32[2,256]{1,0:T(2,128)S(1)}, ...), condition=%wide.region_11.12_spmd, body=%wide.region_8.11_spmd.sunk | while | flops 554174464 | bytes 38162012 | solution.py:46
  299.9 22.3 %psum.37 = f32[512]{0:T(512)S(1)} all-reduce(f32[512]{0:T(512)S(1)} %get-tuple-element.716), channel_id=1, replica_groups=mesh['phase'=2,'seq'=16] {'seq'}, use_global_device_ids=true, to_apply=%region_13.14 | all-reduce | flops 512 | bytes 4096 | tf_op jit(solution)/shard_map/psum | solution.py:93
  331.2 146.1 %while.78 = (s32[]{:T(128)}, f32[2048,4,2,64]{0,3,1,2:T(8,128)}, f32[2,256,4,64]{1,0,3,2:T(2,128)}, f32[2,256,4,64]{1,0,3,2:T(2,128)}, bf16[2,256,4,64]{1,3,2,0:...) while((s32[]{:T(128)}, f32[2048,4,2,64]{0,3,1,2:T(8,128)}, ...), condition=%wide.region_22.23_spmd.clone, body=%wide.region_18.22_spmd.clone.sunk | while | flops 1664622592 | bytes 126128272 | solution.py:80
  377.7 15.8 %fusion.354 = f32[2048,4,1,64]{0,3,1,2:T(8,128)S(1)} fusion(f32[4,256,2048]{2,1,0:T(8,128)} %fusion.353, bf16[2,256,4,64]{1,3,2,0:T(8,128)(2,1)} %get-tuple-element.1185, s32[]{:T(128)} %get-tuple-element.1168, f32[4,256,2048]{2,1,0:T(8,128)} %get-tuple-element.1079, f32[4,256]{1,0:T(4,128)S(1)} %get-tuple-element.1080), kind=kOutput, calls=%fused_computation.82.clone.1 | convolution fusion | flops 283118592 | bytes 35791360 | tf_op jit(solution)/shard_map/while/body/eval_jaxpr/hre,rhd->ehd/dot_general | solution.py:74
  430.1 13.1 %fusion.355 = f32[1,256,4,64]{1,3,2,0:T(8,128)S(1)} fusion(bf16[2048,4,64]{0,2,1:T(8,128)(2,1)} %get-tuple-element.1191, f32[4,256,2048]{2,1,0:T(8,128)} %fusion.353, f32[4,256,2048]{2,1,0:T(8,128)} %get-tuple-element.1079, f32[4,256]{1,0:T(4,128)S(1)} %get-tuple-element.1080), kind=kOutput, calls=%fused_computation.87.clone.1 | convolution fusion | flops 283118592 | bytes 18092032 | tf_op jit(solution)/shard_map/while/body/eval_jaxpr/hre,ehd->rhd/dot_general | solution.py:71
  449.9 15.8 %fusion.354 = f32[2048,4,1,64]{0,3,1,2:T(8,128)S(1)} fusion(f32[4,256,2048]{2,1,0:T(8,128)} %fusion.353, bf16[2,256,4,64]{1,3,2,0:T(8,128)(2,1)} %get-tuple-element.1185, s32[]{:T(128)} %get-tuple-element.1168, f32[4,256,2048]{2,1,0:T(8,128)} %get-tuple-element.1079, f32[4,256]{1,0:T(4,128)S(1)} %get-tuple-element.1080), kind=kOutput, calls=%fused_computation.82.clone.1 | convolution fusion | flops 283118592 | bytes 35791360 | tf_op jit(solution)/shard_map/while/body/eval_jaxpr/hre,rhd->ehd/dot_general | solution.py:74
  482.3 27.9 %psum.38 = f32[512]{0:T(512)S(1)} all-reduce(f32[512]{0:T(512)S(1)} %bitcast.455), channel_id=1, replica_groups=mesh['phase'=2,'seq'=16] {'seq'}, use_global_device_ids=true, to_apply=%region_24.25 | all-reduce | flops 512 | bytes 4096 | tf_op jit(solution)/shard_map/psum | solution.py:113
  527.5 146.1 %while.79 = (s32[]{:T(128)}, f32[2048,4,2,64]{0,3,1,2:T(8,128)}, f32[2,256,4,64]{1,0,3,2:T(2,128)}, f32[2,256,4,64]{1,0,3,2:T(2,128)}, bf16[2,256,4,64]{1,3,2,0:...) while((s32[]{:T(128)}, f32[2048,4,2,64]{0,3,1,2:T(8,128)}, ...), condition=%wide.region_29.30_spmd.clone, body=%wide.region_25.29_spmd.clone.sunk | while | flops 1664622592 | bytes 126128272 | solution.py:80
  553.8 13.1 %fusion.373 = f32[1,256,4,64]{1,3,2,0:T(8,128)S(1)} fusion(bf16[2048,4,64]{0,2,1:T(8,128)(2,1)} %get-tuple-element.1230, f32[4,256,2048]{2,1,0:T(8,128)} %fusion.371, f32[4,256,2048]{2,1,0:T(8,128)} %get-tuple-element.1092, f32[4,256]{1,0:T(4,128)S(1)} %get-tuple-element.1093), kind=kOutput, calls=%fused_computation.132.clone.1 | convolution fusion | flops 283118592 | bytes 18092032 | tf_op jit(solution)/shard_map/while/body/eval_jaxpr/hre,ehd->rhd/dot_general | solution.py:71
  573.6 15.8 %fusion.372 = f32[2048,4,1,64]{0,3,1,2:T(8,128)S(1)} fusion(f32[4,256,2048]{2,1,0:T(8,128)} %fusion.371, bf16[2,256,4,64]{1,3,2,0:T(8,128)(2,1)} %get-tuple-element.1224, s32[]{:T(128)} %get-tuple-element.1207, f32[4,256,2048]{2,1,0:T(8,128)} %get-tuple-element.1092, f32[4,256]{1,0:T(4,128)S(1)} %get-tuple-element.1093), kind=kOutput, calls=%fused_computation.127.clone.1 | convolution fusion | flops 283118592 | bytes 35791360 | tf_op jit(solution)/shard_map/while/body/eval_jaxpr/hre,rhd->ehd/dot_general | solution.py:74
  626.0 13.1 %fusion.373 = f32[1,256,4,64]{1,3,2,0:T(8,128)S(1)} fusion(bf16[2048,4,64]{0,2,1:T(8,128)(2,1)} %get-tuple-element.1230, f32[4,256,2048]{2,1,0:T(8,128)} %fusion.371, f32[4,256,2048]{2,1,0:T(8,128)} %get-tuple-element.1092, f32[4,256]{1,0:T(4,128)S(1)} %get-tuple-element.1093), kind=kOutput, calls=%fused_computation.132.clone.1 | convolution fusion | flops 283118592 | bytes 18092032 | tf_op jit(solution)/shard_map/while/body/eval_jaxpr/hre,ehd->rhd/dot_general | solution.py:71
  645.8 15.8 %fusion.372 = f32[2048,4,1,64]{0,3,1,2:T(8,128)S(1)} fusion(f32[4,256,2048]{2,1,0:T(8,128)} %fusion.371, bf16[2,256,4,64]{1,3,2,0:T(8,128)(2,1)} %get-tuple-element.1224, s32[]{:T(128)} %get-tuple-element.1207, f32[4,256,2048]{2,1,0:T(8,128)} %get-tuple-element.1092, f32[4,256]{1,0:T(4,128)S(1)} %get-tuple-element.1093), kind=kOutput, calls=%fused_computation.127.clone.1 | convolution fusion | flops 283118592 | bytes 35791360 | tf_op jit(solution)/shard_map/while/body/eval_jaxpr/hre,rhd->ehd/dot_general | solution.py:74
  677.1 29.5 %psum.39 = f32[512]{0:T(512)S(1)} all-reduce(f32[512]{0:T(512)S(1)} %bitcast.456), channel_id=1, replica_groups=mesh['phase'=2,'seq'=16] {'seq'}, use_global_device_ids=true, to_apply=%region_31.32 | all-reduce | flops 512 | bytes 4096 | tf_op jit(solution)/shard_map/psum | solution.py:113
  711.7 35.3 %while.77 = (s32[]{:T(128)}, f32[2,256,4,64]{1,0,3,2:T(2,128)S(1)}, s32[2,256]{1,0:T(2,128)S(1)}, s32[2048]{0:T(1024)S(1)}, bf16[2,256,4,64]{1,3,2,0:T(8,128)(2,...) while((s32[]{:T(128)}, f32[2,256,4,64]{1,0,3,2:T(2,128)S(1)}, ...), condition=%wide.region_17.18_spmd, body=%wide.region_14.17_spmd.sunk | while | flops 554174464 | bytes 46550648 | solution.py:46
  760.8 145.7 %while.80 = (s32[]{:T(128)}, f32[2048,4,2,64]{0,3,1,2:T(8,128)}, f32[2,256,4,64]{1,0,3,2:T(2,128)}, f32[2,256,4,64]{1,0,3,2:T(2,128)}, bf16[2,256,4,64]{1,3,2,0:...) while((s32[]{:T(128)}, f32[2048,4,2,64]{0,3,1,2:T(8,128)}, ...), condition=%wide.region_36.37_spmd.clone, body=%wide.region_32.36_spmd.clone.sunk | while | flops 1664622592 | bytes 126128272 | solution.py:80
  787.3 13.1 %fusion.391 = f32[1,256,4,64]{1,3,2,0:T(8,128)S(1)} fusion(bf16[2048,4,64]{0,2,1:T(8,128)(2,1)} %get-tuple-element.1293, f32[4,256,2048]{2,1,0:T(8,128)} %fusion.389, f32[4,256,2048]{2,1,0:T(8,128)} %get-tuple-element.1105, f32[4,256]{1,0:T(4,128)S(1)} %get-tuple-element.1106), kind=kOutput, calls=%fused_computation.177.clone.1 | convolution fusion | flops 283118592 | bytes 18092032 | tf_op jit(solution)/shard_map/while/body/eval_jaxpr/hre,ehd->rhd/dot_general | solution.py:71
  807.1 15.8 %fusion.390 = f32[2048,4,1,64]{0,3,1,2:T(8,128)S(1)} fusion(f32[4,256,2048]{2,1,0:T(8,128)} %fusion.389, bf16[2,256,4,64]{1,3,2,0:T(8,128)(2,1)} %get-tuple-element.1287, s32[]{:T(128)} %get-tuple-element.1270, f32[4,256,2048]{2,1,0:T(8,128)} %get-tuple-element.1105, f32[4,256]{1,0:T(4,128)S(1)} %get-tuple-element.1106), kind=kOutput, calls=%fused_computation.172.clone.1 | convolution fusion | flops 283118592 | bytes 35791360 | tf_op jit(solution)/shard_map/while/body/eval_jaxpr/hre,rhd->ehd/dot_general | solution.py:74
  859.4 13.1 %fusion.391 = f32[1,256,4,64]{1,3,2,0:T(8,128)S(1)} fusion(bf16[2048,4,64]{0,2,1:T(8,128)(2,1)} %get-tuple-element.1293, f32[4,256,2048]{2,1,0:T(8,128)} %fusion.389, f32[4,256,2048]{2,1,0:T(8,128)} %get-tuple-element.1105, f32[4,256]{1,0:T(4,128)S(1)} %get-tuple-element.1106), kind=kOutput, calls=%fused_computation.177.clone.1 | convolution fusion | flops 283118592 | bytes 18092032 | tf_op jit(solution)/shard_map/while/body/eval_jaxpr/hre,ehd->rhd/dot_general | solution.py:71
  879.2 15.8 %fusion.390 = f32[2048,4,1,64]{0,3,1,2:T(8,128)S(1)} fusion(f32[4,256,2048]{2,1,0:T(8,128)} %fusion.389, bf16[2,256,4,64]{1,3,2,0:T(8,128)(2,1)} %get-tuple-element.1287, s32[]{:T(128)} %get-tuple-element.1270, f32[4,256,2048]{2,1,0:T(8,128)} %get-tuple-element.1105, f32[4,256]{1,0:T(4,128)S(1)} %get-tuple-element.1106), kind=kOutput, calls=%fused_computation.172.clone.1 | convolution fusion | flops 283118592 | bytes 35791360 | tf_op jit(solution)/shard_map/while/body/eval_jaxpr/hre,rhd->ehd/dot_general | solution.py:74
  924.1 19.0 %all-to-all-start.1 = ((bf16[2,2048,512]{2,0,1:T(2,128)(2,1)}), bf16[2,2048,512]{2,0,1:T(2,128)(2,1)}, u32[]{:S(2)}, u32[]{:S(2)}) async-start(bf16[2,2048,512]{2,0,1:T(2,128)(2,1)} %copy.158), calls=%async_computation.1 | async-start | bytes 8388608 | tf_op jit(solution)/shard_map/all_to_all | solution.py:176
  950.3 85.3 %all-to-all-done.1 = bf16[2,2048,512]{2,0,1:T(2,128)(2,1)} async-done(((bf16[2,2048,512]{2,0,1:T(2,128)(2,1)}), bf16[2,2048,512]{2,0,1:T(2,128)(2,1)}, u32[]{:S(2)}, u32[]{:S(2)}) %all-to-all-start.1) | async-done | bytes 4194336 | tf_op jit(solution)/shard_map/all_to_all | solution.py:176
  (392 shorter events, 573.9 us)
Async XLA Ops:
  0.7 127.5 %copy-start.56 = (f32[1,256]{1,0:T(1,128)S(1)}, f32[1,256]{1,0:T(1,128)}, u32[]{:S(2)}) copy-start(f32[1,256]{1,0:T(1,128)} %param.23) | copy-start | bytes 3076
  11.9 118.9 %copy-start.28 = (bf16[2,512,256]{2,1,0:T(8,128)(2,1)S(1)}, bf16[2,512,256]{2,1,0:T(8,128)(2,1)}, u32[]{:S(2)}) copy-start(bf16[2,512,256]{2,1,0:T(8,128)(2,1)} %param.25) | copy-start | bytes 1572868
  11.9 119.5 %copy-start.39 = (f32[1,256]{1,0:T(1,128)S(1)}, f32[1,256]{1,0:T(1,128)}, u32[]{:S(2)}) copy-start(f32[1,256]{1,0:T(1,128)} %param.24) | copy-start | bytes 3076
  11.9 122.8 %copy-start.33 = (s32[2,2048]{1,0:T(2,128)S(1)}, s32[2,2048]{1,0:T(2,128)}, u32[]{:S(2)}) copy-start(s32[2,2048]{1,0:T(2,128)} %param.22) | copy-start | bytes 49156
  11.9 124.5 %all-to-all-start = ((bf16[2,128,8192]{1,0,2:T(2,128)(2,1)}), bf16[2,128,8192]{1,0,2:T(2,128)(2,1)}, u32[]{:S(2)}, u32[]{:S(2)}) async-start(bf16[2,128,8192]{1,0,2:T(2,128)(2,1)} %bitcast.407), calls=%async_computation | async-start | bytes 8388608 | tf_op jit(solution)/shard_map/all_to_all | solution.py:129
  193.9 26.9 %collective-permute-start = (bf16[512,256]{0,1:T(8,128)(2,1)}, bf16[512,256]{0,1:T(8,128)(2,1)}, u32[]{:S(2)}, u32[]{:S(2)}) collective-permute-start(bf16[512,256]{0,1:T(8,128)(2,1)} %fusion.213), channel_id=1, source_target_pairs={{0,16},{1,17},{2,18},{3,19},{4,20},{5,21},{6,22},{7,23},{8,24},{9,... | collective-permute-start | bytes 786440 | tf_op jit(solution)/shard_map/ppermute | solution.py:20
  281.8 17.1 %collective-permute-start.1 = (bf16[512,256]{0,1:T(8,128)(2,1)}, bf16[512,256]{0,1:T(8,128)(2,1)}, u32[]{:S(2)}, u32[]{:S(2)}) collective-permute-start(bf16[512,256]{0,1:T(8,128)(2,1)} %get-tuple-element.715), channel_id=1, source_target_pairs={{0,16},{1,17},{2,18},{3,19},{4,20},{5,21},{6,22},{7,23},{8,24},{9,... | collective-permute-start | bytes 786440 | tf_op jit(solution)/shard_map/ppermute | solution.py:20
  331.2 146.2 %copy-start.62 = (f32[512]{0:T(512)S(1)}, f32[512]{0:T(512)}, u32[]{:S(2)}) copy-start(f32[512]{0:T(512)} %get-tuple-element.710) | copy-start | bytes 6148
  331.2 147.6 %copy-start.36 = (f32[4,64]{1,0:T(4,128)S(1)}, f32[4,64]{1,0:T(4,128)}, u32[]{:S(2)}) copy-start(f32[4,64]{1,0:T(4,128)} %copy-done.34) | copy-start | bytes 3076
  331.2 180.1 %copy-start.46 = (f32[1,512]{1,0:T(1,128)S(1)}, f32[1,512]{1,0:T(1,128)}, u32[]{:S(2)}) copy-start(f32[1,512]{1,0:T(1,128)} %get-tuple-element.763) | copy-start | bytes 6148
  331.2 180.2 %copy-start.57 = (f32[1,256]{1,0:T(1,128)S(1)}, f32[1,256]{1,0:T(1,128)}, u32[]{:S(2)}) copy-start(f32[1,256]{1,0:T(1,128)} %param.23) | copy-start | bytes 3076
  331.2 183.5 %copy-start.61 = (f32[512]{0:T(512)S(1)}, f32[512]{0:T(512)}, u32[]{:S(2)}) copy-start(f32[512]{0:T(512)} %get-tuple-element.761) | copy-start | bytes 6148
  512.5 11.4 %collective-permute-start.2 = (bf16[512,256]{0,1:T(8,128)(2,1)S(1)}, bf16[512,256]{0,1:T(8,128)(2,1)S(1)}, u32[]{:S(2)}, u32[]{:S(2)}) collective-permute-start(bf16[512,256]{0,1:T(8,128)(2,1)S(1)} %fusion.211), channel_id=1, source_target_pairs={{16,0},{17,1},{18,2},{19,3},{20,4},{21,5},{22,6},{23,7},{24,8},{25... | collective-permute-start | bytes 786440 | tf_op jit(solution)/shard_map/ppermute | solution.py:20
  527.4 146.2 %copy-start.37 = (f32[4,64]{1,0:T(4,128)S(1)}, f32[4,64]{1,0:T(4,128)}, u32[]{:S(2)}) copy-start(f32[4,64]{1,0:T(4,128)} %copy-done.34) | copy-start | bytes 3076
  527.4 146.2 %copy-start.51 = (f32[2,256]{1,0:T(2,128)S(1)}, f32[2,256]{1,0:T(2,128)}, u32[]{:S(2)}) copy-start(f32[2,256]{1,0:T(2,128)} %rsqrt.62) | copy-start | bytes 6148
  527.4 146.2 %copy-start.55 = (f32[2,256]{1,0:T(2,128)S(1)}, f32[2,256]{1,0:T(2,128)}, u32[]{:S(2)}) copy-start(f32[2,256]{1,0:T(2,128)} %copy-done.54) | copy-start | bytes 6148
  527.4 181.3 %copy-start.48 = (f32[1,512]{1,0:T(1,128)S(1)}, f32[1,512]{1,0:T(1,128)}, u32[]{:S(2)}) copy-start(f32[1,512]{1,0:T(1,128)} %copy-done.47) | copy-start | bytes 6148
  527.4 181.3 %copy-start.58 = (f32[1,256]{1,0:T(1,128)S(1)}, f32[1,256]{1,0:T(1,128)}, u32[]{:S(2)}) copy-start(f32[1,256]{1,0:T(1,128)} %param.23) | copy-start | bytes 3076
  527.4 181.3 %copy-start.59 = (f32[512]{0:T(512)S(1)}, f32[512]{0:T(512)}, u32[]{:S(2)}) copy-start(f32[512]{0:T(512)} %get-tuple-element.769) | copy-start | bytes 6148
  527.4 181.3 %copy-start.60 = (f32[512]{0:T(512)S(1)}, f32[512]{0:T(512)}, u32[]{:S(2)}) copy-start(f32[512]{0:T(512)} %get-tuple-element.770) | copy-start | bytes 6148
  527.4 184.3 %copy-start.30 = (s32[1,2048]{1,0:T(1,128)S(1)}, s32[1,2048]{1,0:T(1,128)}, u32[]{:S(2)}) copy-start(s32[1,2048]{1,0:T(1,128)} %get-tuple-element.757) | copy-start | bytes 24580
  527.4 184.3 %copy-start.43 = (s32[2,256]{1,0:T(2,128)S(1)}, s32[2,256]{1,0:T(2,128)}, u32[]{:S(2)}) copy-start(s32[2,256]{1,0:T(2,128)} %reshape.571) | copy-start | bytes 6148
  747.1 9.1 collective-permute-start.3
  924.1 111.5 %all-to-all-start.1 = ((bf16[2,2048,512]{2,0,1:T(2,128)(2,1)}), bf16[2,2048,512]{2,0,1:T(2,128)(2,1)}, u32[]{:S(2)}, u32[]{:S(2)}) async-start(bf16[2,2048,512]{2,0,1:T(2,128)(2,1)} %copy.158), calls=%async_computation.1 | async-start | bytes 8388608 | tf_op jit(solution)/shard_map/all_to_all | solution.py:176
  (49 other events, 914.8 us)
where the time goes:
time: 1070 us; the launch traced here: 1050 us
  matrix products  323 us (30%)
  local copies, waits for them, and re-layouts  249 us (23%)
  blocking collectives  211 us (20%)
  other arithmetic  146 us (14%)
  waiting for transfers between devices  85.9 us (8%)
  starting transfers between devices  34.8 us (3%)
    psum x3, blocking collectives, section_forward(): total = lax.psum(jnp.sum(xf * xf, axis=1), 'seq')  153 us
    dynamic_update_slice x36, local copies, waits for them, and re-layouts, attend_rows(): output = lax.map(one_block, (query_blocks, seg_blocks))  103 us
    dot_general x6, matrix products, one_block(): jnp.einsum('hre,rhd->ehd', grad_scores, qblock, preferred_element_type=jn...  94.8 us
    all_to_all x1, waiting for transfers between devices, local(): lax.all_to_all(grad_buf, 'seq', split_axis=1, concat_axis=2, tiled=True)  85.3 us
    dot_general x6, matrix products, one_block(): jnp.einsum('hre,ehd->rhd', grad_scores, keys, preferred_element_type=jnp....  78.8 us
    sub x12, other arithmetic, attend(): expo = jnp.exp(scores - top)  71.2 us
    dot_general x12, matrix products, attend(): jnp.einsum('hre,ehd->rhd', weights, values, preferred_element_type=jnp.fl...  59.8 us
    psum x2, blocking collectives, section_backward(): cross = lax.psum(jnp.sum(grad_normed * xf, axis=1), 'seq')  57.4 us
  transfers between devices with their start and end apart: 6, of which 2 were waited for; matrix products, arithmetic and copies ran while one was open for 7% of the time, Pallas kernels for 0%

commit v1 on v0

v1 whole, which is shorter than its diff:
```python
import functools

import jax
import jax.numpy as jnp
from jax import lax
from jax.experimental import pallas as pl
from jax.experimental.pallas import tpu as pltpu
from jax.sharding import PartitionSpec as P

HEAD = 64
QROWS = 256
CHUNK = 256
SCALE = 0.125

eps = 1e-06
neg_big = -1e30
MESH = pl.DeviceIdType.MESH
VMEM_BYTES = 56 * 1024 * 1024


def matmul(a, b):
    return lax.dot_general(a, b, (((1,), (0,)), ((), ())), preferred_element_type=jnp.float32)


def matmul_t(a, b):
    return lax.dot_general(a, b, (((1,), (1,)), ((), ())), preferred_element_type=jnp.float32)


def attention_kernel(backward, active, width, *refs):
    if backward:
        (phase_ref, bound_ref, kv_ref, kseg_ref, qseg_ref, x_ref, total_ref, qg_ref, og_ref, g_ref,
         y_ref, gkv_ref, part_ref, cross_ref, gqg_ref, gog_ref,
         score_ref, top_ref, kvt_ref, pair_ref, gprob_ref, acc_ref) = refs
    else:
        (phase_ref, bound_ref, kv_ref, kseg_ref, qseg_ref, x_ref, total_ref, qg_ref, og_ref,
         y_ref, score_ref, top_ref, kvt_ref, pair_ref) = refs
    enc = kv_ref.shape[0]
    feats, rows = x_ref.shape
    heads = feats // HEAD
    block = min(QROWS, rows)
    chunk = min(CHUNK, enc)
    every = range(heads)
    lanes = [slice(2 * HEAD * h, 2 * HEAD * (h + 1)) for h in every]
    owns = [slice(HEAD * h, HEAD * (h + 1)) for h in every]

    def place(c):
        return pl.ds(pl.multiple_of(c * chunk, chunk), chunk)

    def work():
        def turn(c, _):
            at = place(c)
            for h in every:
                kvt_ref[h, :, at] = kv_ref[at, lanes[h]].T
                if backward:
                    acc_ref[h, at, :] = jnp.zeros((chunk, 2 * HEAD), jnp.float32)
            return 0

        lax.fori_loop(0, enc // chunk, turn, 0)
        row = jnp.zeros((1, block), jnp.float32)
        tall = jnp.zeros((2 * HEAD, block), jnp.float32)
        blank = jnp.zeros((HEAD, block), jnp.bfloat16)
        for b in range(rows // block):
            cols = slice(b * block, (b + 1) * block)
            low = bound_ref[2 * b]
            high = bound_ref[2 * b + 1]
            inv = lax.rsqrt(total_ref[:, cols] / width + eps)
            qseg = qseg_ref[:, cols]

            def normed_of(h):
                return x_ref[owns[h], cols].astype(jnp.float32) * inv

            for h in every:
                query = (normed_of(h) * qg_ref[owns[h], :]).astype(jnp.bfloat16)
                scaled = (query.astype(jnp.float32) * SCALE).astype(jnp.bfloat16)
                pair_ref[h, :, :block] = jnp.concatenate([scaled, blank], axis=0)
                if backward:
                    grad = (g_ref[owns[h], cols].astype(jnp.float32) * og_ref[owns[h], :]).astype(jnp.bfloat16)
                    pair_ref[h, :, block:] = jnp.concatenate([blank, grad], axis=0)

            def scores(c, carry):
                at = place(c)
                allowed = kseg_ref[at, :] == qseg
                found = []
                for h in every:
                    top, total = carry[h]
                    s = matmul(kv_ref[at, lanes[h]], pair_ref[h, :, :block])
                    s = jnp.where(allowed, s, neg_big)
                    higher = jnp.maximum(top, jnp.max(s, axis=0, keepdims=True))
                    e = jnp.exp(s - higher)
                    score_ref[h, at, :] = e
                    top_ref[h, pl.ds(c, 1), :] = higher
                    found.append((higher, total * jnp.exp(top - higher) + jnp.sum(e, axis=0, keepdims=True)))
                return tuple(found)

            found = lax.fori_loop(low, high, scores, tuple((row + neg_big, row) for h in every))
            tops = [top for top, _ in found]
            shares = [1.0 / total for _, total in found]

            def probs_of(h, c, at):
                return score_ref[h, at, :] * (jnp.exp(top_ref[h, pl.ds(c, 1), :] - tops[h]) * shares[h])

            if not backward:
                def outputs(c, outs):
                    at = place(c)
                    return tuple(
                        outs[h] + matmul(kvt_ref[h, :, at], probs_of(h, c, at).astype(jnp.bfloat16)) for h in every
                    )

                outs = lax.fori_loop(low, high, outputs, tuple(tall for h in every))
                for h in every:
                    xf = x_ref[owns[h], cols].astype(jnp.float32)
                    y_ref[owns[h], cols] = (xf + og_ref[owns[h], :] * outs[h][HEAD:]).astype(jnp.bfloat16)
                continue

            def outputs_and_delta(c, carry):
                at = place(c)
                found = []
                for h in every:
                    out, delta = carry[h]
                    probs = probs_of(h, c, at)
                    score_ref[h, at, :] = probs
                    gprob = matmul(kv_ref[at, lanes[h]], pair_ref[h, :, block:])
                    gprob_ref[h, at, :] = gprob
                    out = out + matmul(kvt_ref[h, :, at], probs.astype(jnp.bfloat16))
                    found.append((out, delta + jnp.sum(probs * gprob, axis=0, keepdims=True)))
                return tuple(found)

            found = lax.fori_loop(low, high, outputs_and_delta, tuple((tall, row) for h in every))
            outs = [out for out, _ in found]
            deltas = [delta for _, delta in found]

            def gradients(c, gqs):
                at = place(c)
                found = []
                for h in every:
                    probs = score_ref[h, at, :]
                    gscore = (probs * (gprob_ref[h, at, :] - deltas[h])).astype(jnp.bfloat16)
                    both = jnp.concatenate([gscore, probs.astype(jnp.bfloat16)], axis=1)
                    acc_ref[h, at, :] += matmul_t(both, pair_ref[h])
                    found.append(gqs[h] + matmul(kvt_ref[h, :, at], gscore))
                return tuple(found)

            gqs = lax.fori_loop(low, high, gradients, tuple(tall for h in every))
            cross = row
            for h in every:
                own = owns[h]
                xf = x_ref[own, cols].astype(jnp.float32)
                gf = g_ref[own, cols].astype(jnp.float32)
                out = outs[h][HEAD:]
                gq = gqs[h][:HEAD] * SCALE
                gn = gq * qg_ref[own, :]
                y_ref[own, cols] = (xf + og_ref[own, :] * out).astype(jnp.bfloat16)
                part_ref[own, cols] = gf + inv * gn
                cross = cross + jnp.sum(gn * xf, axis=0, keepdims=True)
                gqg = jnp.sum(gq * normed_of(h), axis=1, keepdims=True)
                gog = jnp.sum(gf * out, axis=1, keepdims=True)
                gqg_ref[own, :] = gqg if b == 0 else gqg_ref[own, :] + gqg
                gog_ref[own, :] = gog if b == 0 else gog_ref[own, :] + gog
            cross_ref[:, cols] = cross
        if backward:
            def store(c, _):
                at = place(c)
                for h in every:
                    gkv_ref[at, lanes[h]] = acc_ref[h, at, :].astype(jnp.bfloat16)
                return 0

            lax.fori_loop(0, enc // chunk, store, 0)

    pl.when(phase_ref[0] == active)(work)


def attention(backward, active, width, phase, bounds, kv, kseg, qseg, x, total, qg, og, g=None):
    enc = kv.shape[0]
    feats, rows = x.shape
    block = min(QROWS, rows)
    shapes = [jax.ShapeDtypeStruct((feats, rows), jnp.bfloat16)]
    heads = feats // HEAD
    scratch = [
        pltpu.VMEM((heads, enc, block), jnp.float32),
        pltpu.VMEM((heads, max(8, enc // min(CHUNK, enc)), block), jnp.float32),
        pltpu.VMEM((heads, 2 * HEAD, enc), jnp.bfloat16),
        pltpu.VMEM((heads, 2 * HEAD, 2 * block if backward else block), jnp.bfloat16),
    ]
    operands = [phase, bounds, kv, kseg, qseg, x, total, qg, og]
    if backward:
        operands.append(g)
        shapes += [
            jax.ShapeDtypeStruct(kv.shape, jnp.bfloat16),
            jax.ShapeDtypeStruct((feats, rows), jnp.float32),
            jax.ShapeDtypeStruct((1, rows), jnp.float32),
            jax.ShapeDtypeStruct((feats, 1), jnp.float32),
            jax.ShapeDtypeStruct((feats, 1), jnp.float32),
        ]
        scratch += [
            pltpu.VMEM((heads, enc, block), jnp.float32),
            pltpu.VMEM((heads, enc, 2 * HEAD), jnp.float32),
        ]
    smem = pl.BlockSpec(memory_space=pltpu.SMEM)
    vmem = pl.BlockSpec(memory_space=pltpu.VMEM)
    return pl.pallas_call(
        functools.partial(attention_kernel, backward, active, width),
        out_shape=shapes,
        in_specs=[smem, smem] + [vmem] * (len(operands) - 2),
        out_specs=[vmem] * len(shapes),
        scratch_shapes=scratch,
        compiler_params=pltpu.CompilerParams(vmem_limit_bytes=VMEM_BYTES),
        cost_estimate=pl.CostEstimate(
            flops=(12 if backward else 4) * rows * enc * feats, bytes_accessed=4 * kv.size, transcendentals=rows * enc
        ),
        name="section_back" if backward else "section_ahead",
    )(*operands)


def totals_kernel(n, part_ref, total_ref, held, send_sem, recv_sem):
    me = lax.axis_index("seq")
    barrier = pltpu.get_barrier_semaphore()

    def greet(k, _):
        pl.semaphore_signal(barrier, inc=1, device_id={"seq": lax.rem(me + k, n)}, device_id_type=MESH)
        return 0

    lax.fori_loop(1, n, greet, 0)
    pl.semaphore_wait(barrier, n - 1)

    def copy(k, slot):
        return pltpu.make_async_remote_copy(
            src_ref=part_ref, dst_ref=held.at[slot], send_sem=send_sem.at[k], recv_sem=recv_sem.at[slot],
            device_id={"seq": lax.rem(me + k, n)}, device_id_type=MESH,
        )

    def send(k, _):
        copy(k, me).start()
        return 0

    lax.fori_loop(1, n, send, 0)

    def take(k, total):
        source = lax.rem(me + k, n)
        copy(k, source).wait_recv()
        return total + held[source]

    total_ref[...] = lax.fori_loop(1, n, take, part_ref[...])

    def finish(k, _):
        copy(k, me).wait_send()
        return 0

    lax.fori_loop(1, n, finish, 0)


def totals(n, part):
    vmem = pl.BlockSpec(memory_space=pltpu.VMEM)
    return pl.pallas_call(
        functools.partial(totals_kernel, n),
        out_shape=jax.ShapeDtypeStruct(part.shape, jnp.float32),
        in_specs=[vmem],
        out_specs=vmem,
        scratch_shapes=[
            pltpu.VMEM((n,) + part.shape, jnp.float32),
            pltpu.SemaphoreType.DMA((n,)),
            pltpu.SemaphoreType.DMA((n,)),
        ],
        compiler_params=pltpu.CompilerParams(collective_id=0, has_side_effects=True),
        name="row_totals",
    )(part)


def ahead_kernel(n, y_ref, x_ref, total_ref, part, held, send_sem, recv_sem, y_send, y_recv):
    me = lax.axis_index("seq")
    phase = lax.axis_index("phase")
    barrier = pltpu.get_barrier_semaphore()
    y_copy = pltpu.make_async_remote_copy(
        src_ref=y_ref, dst_ref=x_ref, send_sem=y_send, recv_sem=y_recv,
        device_id={"phase": 1 - phase, "seq": me}, device_id_type=MESH,
    )

    def copy(k, slot):
        return pltpu.make_async_remote_copy(
            src_ref=part, dst_ref=held.at[slot], send_sem=send_sem.at[k], recv_sem=recv_sem.at[slot],
            device_id={"phase": 1 - phase, "seq": lax.rem(me + k, n)}, device_id_type=MESH,
        )

    @pl.when(phase == 1)
    def _():
        def greet(k, _):
            pl.semaphore_signal(
                barrier, inc=1, device_id={"phase": 0, "seq": lax.rem(me + k, n)}, device_id_type=MESH
            )
            return 0

        lax.fori_loop(0, n, greet, 0)

        def take(k, total):
            source = lax.rem(me + k, n)
            copy(k, source).wait_recv()
            return total + held[source]

        total_ref[...] = lax.fori_loop(0, n, take, jnp.zeros(total_ref.shape, jnp.float32))
        y_copy.wait_recv()

    @pl.when(phase == 0)
    def _():
        yf = y_ref[...].astype(jnp.float32)
        part[...] = jnp.sum(yf * yf, axis=0, keepdims=True)
        pl.semaphore_wait(barrier, n)
        y_copy.start()

        def send(k, _):
            copy(k, me).start()
            return 0

        lax.fori_loop(0, n, send, 0)

        def finish(k, _):
            copy(k, me).wait_send()
            return 0

        lax.fori_loop(0, n, finish, 0)
        y_copy.wait_send()


def ahead(n, y):
    vmem = pl.BlockSpec(memory_space=pltpu.VMEM)
    rows = y.shape[1]
    return pl.pallas_call(
        functools.partial(ahead_kernel, n),
        out_shape=[jax.ShapeDtypeStruct(y.shape, y.dtype), jax.ShapeDtypeStruct((1, rows), jnp.float32)],
        in_specs=[vmem],
        out_specs=[vmem, vmem],
        scratch_shapes=[
            pltpu.VMEM((1, rows), jnp.float32),
            pltpu.VMEM((n, 1, rows), jnp.float32),
            pltpu.SemaphoreType.DMA((n,)),
            pltpu.SemaphoreType.DMA((n,)),
            pltpu.SemaphoreType.DMA,
            pltpu.SemaphoreType.DMA,
        ],
        compiler_params=pltpu.CompilerParams(collective_id=1, has_side_effects=True),
        name="relay_ahead",
    )(y)


def back_kernel(n, width, part_ref, cross_ref, x_ref, total_ref, g_ref, held, grad, send_sem, recv_sem, g_send, g_recv):
    me = lax.axis_index("seq")
    phase = lax.axis_index("phase")
    barrier = pltpu.get_barrier_semaphore()
    g_copy = pltpu.make_async_remote_copy(
        src_ref=grad, dst_ref=g_ref, send_sem=g_send, recv_sem=g_recv,
        device_id={"phase": 1 - phase, "seq": me}, device_id_type=MESH,
    )

    def copy(k, slot):
        return pltpu.make_async_remote_copy(
            src_ref=cross_ref, dst_ref=held.at[slot], send_sem=send_sem.at[k], recv_sem=recv_sem.at[slot],
            device_id={"phase": phase, "seq": lax.rem(me + k, n)}, device_id_type=MESH,
        )

    @pl.when(phase == 0)
    def _():
        pl.semaphore_signal(barrier, inc=1, device_id={"phase": 1, "seq": me}, device_id_type=MESH)
        g_copy.wait_recv()

    @pl.when(phase == 1)
    def _():
        def greet(k, _):
            pl.semaphore_signal(
                barrier, inc=1, device_id={"phase": 1, "seq": lax.rem(me + k, n)}, device_id_type=MESH
            )
            return 0

        lax.fori_loop(1, n, greet, 0)
        pl.semaphore_wait(barrier, n)

        def send(k, _):
            copy(k, me).start()
            return 0

        lax.fori_loop(1, n, send, 0)

        def take(k, total):
            source = lax.rem(me + k, n)
            copy(k, source).wait_recv()
            return total + held[source]

        cross = lax.fori_loop(1, n, take, cross_ref[...])
        inv = lax.rsqrt(total_ref[...] / width + eps)
        factor = inv * inv * inv * (cross / width)
        grad[...] = (part_ref[...] - x_ref[...].astype(jnp.float32) * factor).astype(jnp.bfloat16)
        g_copy.start()

        def finish(k, _):
            copy(k, me).wait_send()
            return 0

        lax.fori_loop(1, n, finish, 0)
        g_copy.wait_send()


def back(n, width, part, cross, x, total):
    vmem = pl.BlockSpec(memory_space=pltpu.VMEM)
    rows = x.shape[1]
    return pl.pallas_call(
        functools.partial(back_kernel, n, width),
        out_shape=jax.ShapeDtypeStruct(x.shape, jnp.bfloat16),
        in_specs=[vmem] * 4,
        out_specs=vmem,
        scratch_shapes=[
            pltpu.VMEM((n, 1, rows), jnp.float32),
            pltpu.VMEM(x.shape, jnp.bfloat16),
            pltpu.SemaphoreType.DMA((n,)),
            pltpu.SemaphoreType.DMA((n,)),
            pltpu.SemaphoreType.DMA,
            pltpu.SemaphoreType.DMA,
        ],
        compiler_params=pltpu.CompilerParams(collective_id=2, has_side_effects=True),
        name="relay_back",
    )(part, cross, x, total)


def doc_bounds(qseg, kseg):
    block = min(QROWS, qseg.shape[0])
    chunk = min(CHUNK, kseg.shape[0])
    blocks = qseg.reshape(-1, block)
    below = jnp.sum(kseg[None, :] < blocks[:, :1], axis=1)
    upto = jnp.sum(kseg[None, :] <= blocks[:, -1:], axis=1)
    return jnp.stack([below // chunk, (upto + chunk - 1) // chunk], axis=1).reshape(-1).astype(jnp.int32)


def local(n, dec_in, enc_kv, dec_seg, enc_seg, q_gain, o_gain, cotangent):
    phase = lax.axis_index("phase")
    micro, rows, feats = dec_in.shape
    own_enc = enc_kv.shape[2]
    enc = enc_seg.shape[1]
    width = feats * n
    flag = phase.astype(jnp.int32).reshape(1)
    qg = q_gain.reshape(feats, 1)
    og = o_gain.reshape(feats, 1)
    inputs = dec_in.transpose(0, 2, 1)
    wanted = cotangent.transpose(0, 2, 1)
    xf = inputs.astype(jnp.float32)
    first_totals = totals(n, jnp.sum(xf * xf, axis=1))
    scattered = []
    for m in range(micro):
        blocks = enc_kv[0, m].reshape(own_enc, n, 2 * feats).transpose(1, 0, 2)
        if m > 0:
            blocks, scattered[-1], first_totals = lax.optimization_barrier((blocks, scattered[-1], first_totals))
        scattered.append(lax.all_to_all(blocks, "seq", split_axis=0, concat_axis=0, tiled=True))

    calls, x0s, t0s = [], [], []
    for m in range(micro):
        calls.append(functools.partial(
            attention, width=width, phase=flag, bounds=doc_bounds(dec_seg[m], enc_seg[m]),
            kv=scattered[m].reshape(enc, 2 * feats), kseg=enc_seg[m].reshape(enc, 1),
            qseg=dec_seg[m].reshape(1, rows), qg=qg, og=og,
        ))
        x0s.append(inputs[m])
        t0s.append(first_totals[m].reshape(1, rows))
    outs, grads, gqgs, gogs = [], [], [], []

    def finish(m, y0, first, g0):
        y1, gkv1, gqg1, gog1 = first
        _, gkv0, _, _, gqg0, gog0 = calls[m](True, 0, x=x0s[m], total=t0s[m], g=g0)
        outs.append(jnp.where(phase == 0, y0, y1).T)
        grads.append(jnp.where(phase == 0, gkv0, gkv1).reshape(n, own_enc, 2 * feats))
        gqgs.append(jnp.where(phase == 0, gqg0, gqg1))
        gogs.append(jnp.where(phase == 0, gog0, gog1))

    y0 = calls[0](False, 0, x=x0s[0], total=t0s[0])[0]
    waiting = None
    for m in range(micro):
        x1, total1 = ahead(n, y0)
        if waiting is not None:
            x1, waiting[2] = lax.optimization_barrier((x1, waiting[2]))
        y1, gkv1, part, cross, gqg1, gog1 = calls[m](True, 1, x=x1, total=total1, g=wanted[m])
        if waiting is not None:
            waiting[2], part = lax.optimization_barrier((waiting[2], part))
            finish(m - 1, *waiting)
        later = None
        if m + 1 < micro:
            x_next, part = lax.optimization_barrier((x0s[m + 1], part))
            later = calls[m + 1](False, 0, x=x_next, total=t0s[m + 1])[0]
            cross, later = lax.optimization_barrier((cross, later))
        g0 = back(n, width, part, cross, x1, total1)
        if grads:
            grads[-1], g0 = lax.optimization_barrier((grads[-1], g0))
        if later is not None:
            later, g0 = lax.optimization_barrier((later, g0))
        waiting = [y0, (y1, gkv1, gqg1, gog1), g0]
        y0 = later
    finish(micro - 1, *waiting)
    returned = []
    for m in range(micro):
        rows_back = lax.all_to_all(grads[m], "seq", split_axis=0, concat_axis=0, tiled=True)
        returned.append(rows_back.transpose(1, 0, 2).reshape(own_enc, 2 * feats * n))
    return (
        jnp.stack(outs)[None],
        jnp.stack(returned)[None],
        sum(gqgs).reshape(1, feats),
        sum(gogs).reshape(1, feats),
    )


def solution(mesh):
    in_specs = (
        P(None, None, "seq"),
        P("phase", None, "seq", None),
        P(),
        P(),
        P("phase", "seq"),
        P("phase", "seq"),
        P(None, None, "seq"),
    )
    out_specs = (
        P("phase", None, None, "seq"),
        P("phase", None, "seq", None),
        P("phase", "seq"),
        P("phase", "seq"),
    )
    body = functools.partial(local, mesh.shape["seq"])
    return jax.shard_map(body, mesh=mesh, in_specs=in_specs, out_specs=out_specs, check_vma=False)
```

time: 1070 us -> 364 us (0.34); the launches traced: 1050 us -> 364 us
  matrix products: 323 us -> 0 us
  local copies, waits for them, and re-layouts: 249 us -> 37.5 us
  Pallas kernels: 0 us -> 206 us
  blocking collectives: 211 us -> 53.6 us
  other arithmetic: 146 us -> 12.6 us
  waiting for transfers between devices: 85.9 us -> 35.6 us
  starting transfers between devices: 34.8 us -> 17.7 us
    dot_general x48 -> x0, matrix products: 323 us -> none  [the longest x6 94.8 us: one_block(): jnp.einsum('hre,rhd->ehd', grad_scores, qblock, preferred_element_type=jn...]
    psum x5 -> x0, blocking collectives: 211 us -> none  [the longest x3 153 us: section_forward(): total = lax.psum(jnp.sum(xf * xf, axis=1), 'seq')]
    pallas_call x0 -> x11, Pallas kernels: none -> 206 us  [the longest x6 80.5 us: attention(): pl.pallas_call(functools.partial(attention_kernel, backward, active, widt...]
    dynamic_update_slice x36 -> x0, local copies, waits for them, and re-layouts: 103 us -> none  [attend_rows(): output = lax.map(one_block, (query_blocks, seg_blocks))]
    sub x12 -> x0, other arithmetic: 71.2 us -> none  [attend(): expo = jnp.exp(scores - top)]
    all_to_all x0 -> x1, blocking collectives: none -> 53.6 us  [local(): lax.all_to_all(grads[m], 'seq', split_axis=0, concat_axis=0, tiled=True)]
    all_to_all x2 -> x3, waiting for transfers between devices: 85.3 us -> 35.6 us  [the longest x1 35.5 us: local(): lax.all_to_all(grads[m], 'seq', split_axis=0, concat_axis=0, tiled=True)]
    dynamic_slice x27 -> x0, local copies, waits for them, and re-layouts: 36.5 us -> none  [the longest x7 28.4 us: local(): kv_now = lax.dynamic_index_in_dim(kv_buf, index, 0, keepdims=False)]
  transfers between devices with their start and end apart: 6 -> 3, of which waited for: 2 -> 1; matrix products, arithmetic and copies ran while one was open for 7% -> 7% of each run, Pallas kernels for 0% -> 24%
where the time goes in v1:
time: 364 us
  Pallas kernels  206 us (57%)
  blocking collectives  53.6 us (15%)
  local copies, waits for them, and re-layouts  37.5 us (10%)
  waiting for transfers between devices  35.6 us (10%)
  starting transfers between devices  17.7 us (5%)
  other arithmetic  12.6 us (3%)
    pallas_call x6, Pallas kernels, attention(): pl.pallas_call(functools.partial(attention_kernel, backward, active, widt...  80.5 us
    all_to_all x1, blocking collectives, local(): lax.all_to_all(grads[m], 'seq', split_axis=0, concat_axis=0, tiled=True)  53.6 us
    pallas_call x1, Pallas kernels, totals(): pl.pallas_call(functools.partial(totals_kernel, n), out_shape=jax.ShapeDt...  49.2 us
    pallas_call x2, Pallas kernels, back(): pl.pallas_call(functools.partial(back_kernel, n, width), out_shape=jax.Sh...  44.6 us
    all_to_all x1, waiting for transfers between devices, local(): lax.all_to_all(grads[m], 'seq', split_axis=0, concat_axis=0, tiled=True)  35.5 us
    pallas_call x2, Pallas kernels, ahead(): pl.pallas_call(functools.partial(ahead_kernel, n), out_shape=[jax.ShapeDt...  32.1 us
    all_to_all x2, starting transfers between devices, local(): lax.all_to_all(blocks, 'seq', split_axis=0, concat_axis=0, tiled=True)  12.4 us
    another operation x2, local copies, waits for them, and re-layouts, local(): jnp.stack(returned)[None]  8.6 us
  transfers between devices with their start and end apart: 3, of which 1 were waited for; matrix products, arithmetic and copies ran while one was open for 7% of the time, Pallas kernels for 24%

profile of v1, /device:TPU:13, one launch (start us, length us, event | category | flops | bytes accessed | tf_op | source)
XLA Modules:
  0.0 364.3 jit_solution(13572537964108787101)
XLA Ops:
  0.6 2.6 fusion.4
  4.1 2.5 copy.94
  6.6 6.7 %all-to-all-start = ((bf16[16,128,512]{2,1,0:T(8,128)(2,1)}), bf16[16,128,512]{2,1,0:T(8,128)(2,1)}, u32[]{:S(2)}, u32[]{:S(2)}) async-start(bf16[16,128,512]{2,1,0:T(8,128)(2,1)} %bitcast.88), calls=%async_computation | async-start | bytes 4194304 | tf_op jit(solution)/shard_map/all_to_all | solution.py:447
  14.2 49.2 %row_totals.1 = f32[2,512]{1,0:T(2,128)} custom-call(f32[2,512]{1,0:T(2,128)} %multiply_reduce_fusion.part_ref), custom_call_target="tpu_custom_call" | custom-call | tf_op jit(solution)/shard_map/row_totals/pallas_call | solution.py:253
  64.3 2.5 copy.95
  66.8 5.7 %all-to-all-start.1 = ((bf16[16,128,512]{2,1,0:T(8,128)(2,1)}), bf16[16,128,512]{2,1,0:T(8,128)(2,1)S(1)}, u32[]{:S(2)}, u32[]{:S(2)}) async-start(bf16[16,128,512]{2,1,0:T(8,128)(2,1)} %bitcast.89), calls=%async_computation.1 | async-start | bytes 4194304 | tf_op jit(solution)/shard_map/all_to_all | solution.py:447
  83.6 14.0 %section_ahead.2.y_ref = bf16[256,512]{1,0:T(8,128)(2,1)} custom-call(s32[1]{0:T(128)} %bitcast.refs_0_, s32[4]{0:T(128)} %reshape.248.refs_1_, bf16[2048,512]{1,0:T(8,128)(2,1)} %bitcast.9.refs_2_, s32[2048,1]{1,0:T(8,128)} %copy.61.refs_3_, s32[1,512]{1,0:T(1,128)} %get-tuple-element.109.refs_4_, bf16[256,512]{1,0:T(8,128)(2,1)} %get-tuple-element.101.refs_5_, ...), custom_call_target="tpu_custom_call" | custom-call | flops 1073741824 | bytes 4194304 | tf_op jit(solution)/shard_map/section_ahead/pallas_call | solution.py:200
  97.6 21.9 %relay_ahead.2 = (bf16[256,512]{1,0:T(8,128)(2,1)}, f32[1,512]{1,0:T(1,128)}) custom-call(bf16[256,512]{1,0:T(8,128)(2,1)} %section_ahead.2.y_ref), custom_call_target="tpu_custom_call" | custom-call | tf_op jit(solution)/shard_map/relay_ahead/pallas_call | solution.py:325
  119.5 3.9 %section_back.4 = (bf16[256,512]{1,0:T(8,128)(2,1)}, bf16[2048,512]{1,0:T(8,128)(2,1)}, f32[256,512]{1,0:T(8,128)}, f32[1,512]{1,0:T(1,128)}, f32[256,1]{1,0:T(8,128)}, /*index=5*/f32[256,1]{1,0:T(8,128)}) custom-call(s32[1]{0:T(128)} %bitcast.refs_0_, s32[4]{0:T(128)} %reshape.248.refs_1_, bf16[2048,512]{1,0:T(8,128)(2,1)} %bitcast.9.refs_2_, ...), custom_call_target="tpu_custom_call" | custom-call | flops 3221225472 | bytes 4194304 | tf_op jit(solution)/shard_map/section_back/pallas_call | solution.py:200
  124.7 12.5 %section_ahead.3.y_ref = bf16[256,512]{1,0:T(8,128)(2,1)} custom-call(s32[1]{0:T(128)} %bitcast.refs_0_, s32[4]{0:T(128)} %reshape.252.refs_1_, bf16[2048,512]{1,0:T(8,128)(2,1)} %bitcast.98, s32[2048,1]{1,0:T(8,128)} %copy.71.refs_3_, s32[1,512]{1,0:T(1,128)} %get-tuple-element.108.refs_4_, bf16[256,512]{1,0:T(8,128)(2,1)} %get-tuple-element.49.refs_5_, ...), custom_call_target="tpu_custom_call" | custom-call | flops 1073741824 | bytes 4194304 | tf_op jit(solution)/shard_map/section_ahead/pallas_call | solution.py:200
  137.2 29.5 %relay_back.2.refs_9_ = bf16[256,512]{1,0:T(8,128)(2,1)} custom-call(f32[256,512]{1,0:T(8,128)} %get-tuple-element.51.part_ref, f32[1,512]{1,0:T(1,128)} %get-tuple-element.52.cross_ref, bf16[256,512]{1,0:T(8,128)(2,1)} %get-tuple-element.43.refs_5_.x_ref, f32[1,512]{1,0:T(1,128)} %get-tuple-element.44.refs_6_.total_ref), custom_call_target="tpu_custom_call" | custom-call | tf_op jit(solution)/shard_map/relay_back/pallas_call | solution.py:402
  166.7 10.2 %relay_ahead.3 = (bf16[256,512]{1,0:T(8,128)(2,1)}, f32[1,512]{1,0:T(1,128)}) custom-call(bf16[256,512]{1,0:T(8,128)(2,1)} %section_ahead.3.y_ref), custom_call_target="tpu_custom_call" | custom-call | tf_op jit(solution)/shard_map/relay_ahead/pallas_call | solution.py:325
  176.9 3.7 %section_back.5 = (bf16[256,512]{1,0:T(8,128)(2,1)}, bf16[2048,512]{1,0:T(8,128)(2,1)}, f32[256,512]{1,0:T(8,128)}, f32[1,512]{1,0:T(1,128)}, f32[256,1]{1,0:T(8,128)}, /*index=5*/f32[256,1]{1,0:T(8,128)}) custom-call(s32[1]{0:T(128)} %bitcast.refs_0_, s32[4]{0:T(128)} %reshape.252.refs_1_, bf16[2048,512]{1,0:T(8,128)(2,1)} %bitcast.99, ...), custom_call_target="tpu_custom_call" | custom-call | flops 3221225472 | bytes 4194304 | tf_op jit(solution)/shard_map/section_back/pallas_call | solution.py:200
  180.7 24.5 %section_back.6 = (bf16[256,512]{1,0:T(8,128)(2,1)}, bf16[2048,512]{1,0:T(8,128)(2,1)}, f32[256,512]{1,0:T(8,128)}, f32[1,512]{1,0:T(1,128)}, f32[256,1]{1,0:T(8,128)}, /*index=5*/f32[256,1]{1,0:T(8,128)}) custom-call(s32[1]{0:T(128)} %bitcast.refs_0_, s32[4]{0:T(128)} %reshape.248.refs_1_, bf16[2048,512]{1,0:T(8,128)(2,1)} %bitcast.9.refs_2_, ...), custom_call_target="tpu_custom_call" | custom-call | flops 3221225472 | bytes 4194304 | tf_op jit(solution)/shard_map/section_back/pallas_call | solution.py:200
  205.2 15.1 %relay_back.3.refs_9_ = bf16[256,512]{1,0:T(8,128)(2,1)} custom-call(f32[256,512]{1,0:T(8,128)} %get-tuple-element.64.part_ref, f32[1,512]{1,0:T(1,128)} %get-tuple-element.65.cross_ref, bf16[256,512]{1,0:T(8,128)(2,1)} %get-tuple-element.56.refs_5_.x_ref, f32[1,512]{1,0:T(1,128)} %get-tuple-element.57.refs_6_.total_ref), custom_call_target="tpu_custom_call" | custom-call | tf_op jit(solution)/shard_map/relay_back/pallas_call | solution.py:402
  220.3 3.1 broadcast_select_fusion.1
  223.4 21.9 %section_back.7 = (bf16[256,512]{1,0:T(8,128)(2,1)}, bf16[2048,512]{1,0:T(8,128)(2,1)}, f32[256,512]{1,0:T(8,128)}, f32[1,512]{1,0:T(1,128)}, f32[256,1]{1,0:T(8,128)}, /*index=5*/f32[256,1]{1,0:T(8,128)}) custom-call(s32[1]{0:T(128)} %bitcast.refs_0_, s32[4]{0:T(128)} %reshape.252.refs_1_, bf16[2048,512]{1,0:T(8,128)(2,1)} %bitcast.100, ...), custom_call_target="tpu_custom_call" | custom-call | flops 3221225472 | bytes 4194304 | tf_op jit(solution)/shard_map/section_back/pallas_call | solution.py:200
  247.1 53.6 %all_to_all.20 = bf16[16,128,512]{2,1,0:T(8,128)(2,1)} all-to-all(bf16[16,128,512]{2,1,0:T(8,128)(2,1)S(1)} %bitcast.90), channel_id=1, replica_groups=mesh['phase'=2,'seq'=16] {'seq'}, dimensions={0} | all-to-all | bytes 4194304 | tf_op jit(solution)/shard_map/all_to_all | solution.py:493
  300.7 5.3 %all-to-all-start.2 = ((bf16[16,128,512]{2,1,0:T(8,128)(2,1)}), bf16[16,128,512]{2,1,0:T(8,128)(2,1)S(1)}, u32[]{:S(2)}, u32[]{:S(2)}) async-start(bf16[16,128,512]{2,1,0:T(8,128)(2,1)} %bitcast.30), calls=%async_computation.2 | async-start | bytes 4194304 | tf_op jit(solution)/shard_map/all_to_all | solution.py:493
  309.6 4.1 %copy.84 = bf16[128,16,512]{2,1,0:T(8,128)(2,1)} copy(bf16[128,16,512]{2,0,1:T(8,128)(2,1)} %bitcast.92) | data formatting | bytes 4194304 | tf_op jit(solution)/shard_map/transpose | solution.py:494
  313.6 4.2 %stack_reshape.7 = bf16[1,128,8192]{2,1,0:T(8,128)(2,1)} reshape(bf16[128,16,512]{2,1,0:T(8,128)(2,1)} %copy.84) | data formatting | bytes 4194304 | tf_op jit(solution)/shard_map/stack;reshape | solution.py:497
  317.9 35.5 %all-to-all-done.2 = bf16[16,128,512]{2,1,0:T(8,128)(2,1)S(1)} async-done(((bf16[16,128,512]{2,1,0:T(8,128)(2,1)}), bf16[16,128,512]{2,1,0:T(8,128)(2,1)S(1)}, u32[]{:S(2)}, u32[]{:S(2)}) %all-to-all-start.2) | async-done | bytes 2097184 | tf_op jit(solution)/shard_map/all_to_all | solution.py:493
  355.9 4.4 %stack_reshape.6 = bf16[1,128,8192]{2,1,0:T(8,128)(2,1)} reshape(bf16[128,16,512]{2,1,0:T(8,128)(2,1)} %copy.80) | data formatting | bytes 4194304 | tf_op jit(solution)/shard_map/stack;reshape | solution.py:497
  360.3 4.0 %maximum_bitcast_fusion = bf16[1,2,128,8192]{3,2,1,0:T(8,128)(2,1)} fusion(bf16[1,128,8192]{2,1,0:T(8,128)(2,1)S(1)} %copy-done, bf16[1,128,8192]{2,1,0:T(8,128)(2,1)} %stack_reshape.6), kind=kLoop, calls=%fused_computation | loop fusion | flops 2097152 | bytes 8388608 | tf_op jit(solution)/shard_map/broadcast_in_dim | solution.py:497
  (80 shorter events, 22.7 us)
Async XLA Ops:
  6.6 6.7 %copy-start.6 = (bf16[2,512,256]{2,1,0:T(8,128)(2,1)S(1)}, bf16[2,512,256]{2,1,0:T(8,128)(2,1)}, u32[]{:S(2)}) copy-start(bf16[2,512,256]{2,1,0:T(8,128)(2,1)} %param.7) | copy-start | bytes 1572868
  6.6 60.2 %all-to-all-start = ((bf16[16,128,512]{2,1,0:T(8,128)(2,1)}), bf16[16,128,512]{2,1,0:T(8,128)(2,1)}, u32[]{:S(2)}, u32[]{:S(2)}) async-start(bf16[16,128,512]{2,1,0:T(8,128)(2,1)} %bitcast.88), calls=%async_computation | async-start | bytes 4194304 | tf_op jit(solution)/shard_map/all_to_all | solution.py:447
  66.7 5.8 %copy-start.16 = (s32[2,512]{1,0:T(2,128)S(1)}, s32[2,512]{1,0:T(2,128)}, u32[]{:S(2)}) copy-start(s32[2,512]{1,0:T(2,128)} %param.9) | copy-start | bytes 12292
  66.7 6.9 %copy-start.14 = (s32[2,2048]{1,0:T(2,128)S(1)}, s32[2,2048]{1,0:T(2,128)}, u32[]{:S(2)}) copy-start(s32[2,2048]{1,0:T(2,128)} %param.10) | copy-start | bytes 49156
  66.7 8.9 %copy-start.17 = (f32[1,256]{1,0:T(1,128)S(1)}, f32[1,256]{1,0:T(1,128)}, u32[]{:S(2)}) copy-start(f32[1,256]{1,0:T(1,128)} %param.11) | copy-start | bytes 3076
  66.8 9.7 %copy-start.18 = (f32[1,256]{1,0:T(1,128)S(1)}, f32[1,256]{1,0:T(1,128)}, u32[]{:S(2)}) copy-start(f32[1,256]{1,0:T(1,128)} %param.12) | copy-start | bytes 3076
  66.8 56.6 %all-to-all-start.1 = ((bf16[16,128,512]{2,1,0:T(8,128)(2,1)}), bf16[16,128,512]{2,1,0:T(8,128)(2,1)S(1)}, u32[]{:S(2)}, u32[]{:S(2)}) async-start(bf16[16,128,512]{2,1,0:T(8,128)(2,1)} %bitcast.89), calls=%async_computation.1 | async-start | bytes 4194304 | tf_op jit(solution)/shard_map/all_to_all | solution.py:447
  78.5 4.5 %copy-start.15 = (f32[2,512]{1,0:T(2,128)S(1)}, f32[2,512]{1,0:T(2,128)}, u32[]{:S(2)}) copy-start(f32[2,512]{1,0:T(2,128)} %row_totals.1) | copy-start | bytes 12292
  123.4 1.3 copy-start.3
  180.7 39.6 %copy-start.1 = (bf16[2048,512]{1,0:T(8,128)(2,1)S(1)}, bf16[2048,512]{1,0:T(8,128)(2,1)}, u32[]{:S(2)}) copy-start(bf16[2048,512]{1,0:T(8,128)(2,1)} %get-tuple-element.63) | copy-start | bytes 6291460
  223.4 21.9 %copy-start.2 = (bf16[2048,512]{1,0:T(8,128)(2,1)S(1)}, bf16[2048,512]{1,0:T(8,128)(2,1)}, u32[]{:S(2)}) copy-start(bf16[2048,512]{1,0:T(8,128)(2,1)} %get-tuple-element.69) | copy-start | bytes 6291460
  300.7 5.3 %copy-start.4 = (bf16[256,512]{1,0:T(8,128)(2,1)S(1)}, bf16[256,512]{1,0:T(8,128)(2,1)}, u32[]{:S(2)}) copy-start(bf16[256,512]{1,0:T(8,128)(2,1)} %section_ahead.2.y_ref) | copy-start | bytes 786436
  300.7 5.3 %copy-start.7 = (bf16[256,512]{1,0:T(8,128)(2,1)S(1)}, bf16[256,512]{1,0:T(8,128)(2,1)}, u32[]{:S(2)}) copy-start(bf16[256,512]{1,0:T(8,128)(2,1)} %get-tuple-element.45) | copy-start | bytes 786436
  300.7 5.4 %copy-start.5 = (bf16[256,512]{1,0:T(8,128)(2,1)S(1)}, bf16[256,512]{1,0:T(8,128)(2,1)}, u32[]{:S(2)}) copy-start(bf16[256,512]{1,0:T(8,128)(2,1)} %section_ahead.3.y_ref) | copy-start | bytes 786436
  300.7 5.4 %copy-start.8 = (bf16[256,512]{1,0:T(8,128)(2,1)S(1)}, bf16[256,512]{1,0:T(8,128)(2,1)}, u32[]{:S(2)}) copy-start(bf16[256,512]{1,0:T(8,128)(2,1)} %get-tuple-element.58) | copy-start | bytes 786436
  300.7 52.7 %all-to-all-start.2 = ((bf16[16,128,512]{2,1,0:T(8,128)(2,1)}), bf16[16,128,512]{2,1,0:T(8,128)(2,1)S(1)}, u32[]{:S(2)}, u32[]{:S(2)}) async-start(bf16[16,128,512]{2,1,0:T(8,128)(2,1)} %bitcast.30), calls=%async_computation.2 | async-start | bytes 4194304 | tf_op jit(solution)/shard_map/all_to_all | solution.py:493
  306.0 1.2 copy-start.10
  306.0 2.8 copy-start.9
  306.0 2.8 copy-start.11
  306.1 2.8 copy-start.12
  306.1 2.8 copy-start.13
  355.9 4.4 %copy-start = (bf16[1,128,8192]{2,1,0:T(8,128)(2,1)S(1)}, bf16[1,128,8192]{2,1,0:T(8,128)(2,1)}, u32[]{:S(2)}) copy-start(bf16[1,128,8192]{2,1,0:T(8,128)(2,1)} %stack_reshape.7) | copy-start | bytes 6291460

commit v2 on v1

--- a/solution.py
+++ b/solution.py
@@ -15,7 +15,7 @@
 eps = 1e-06
 neg_big = -1e30
 MESH = pl.DeviceIdType.MESH
-VMEM_BYTES = 56 * 1024 * 1024
+VMEM_BYTES = 36 * 1024 * 1024
 
 
 def matmul(a, b):
@@ -205,7 +205,8 @@
         scratch_shapes=scratch,
         compiler_params=pltpu.CompilerParams(vmem_limit_bytes=VMEM_BYTES),
         cost_estimate=pl.CostEstimate(
-            flops=(12 if backward else 4) * rows * enc * feats, bytes_accessed=4 * kv.size, transcendentals=rows * enc
+            flops=(72 if backward else 32) * rows * enc * feats, bytes_accessed=4 * kv.size,
+            transcendentals=rows * enc * heads,
         ),
         name="section_back" if backward else "section_ahead",
     )(*operands)
@@ -265,156 +266,200 @@
     )(part)
 
 
-def ahead_kernel(n, y_ref, x_ref, total_ref, part, held, send_sem, recv_sem, y_send, y_recv):
+def exchange_kernel(n, width, ahead, back, *refs):
+    refs = list(refs)
+    y_ref = refs.pop(0) if ahead else None
+    part_ref, cross_ref, x_ref, total_ref = [refs.pop(0) for _ in range(4)] if back else [None] * 4
+    x_out, total_out = [refs.pop(0) for _ in range(2)] if ahead else [None] * 2
+    g_out = refs.pop(0) if back else None
+    if ahead:
+        square, held, send_sem, recv_sem, y_send, y_recv = [refs.pop(0) for _ in range(6)]
+    if back:
+        crosses, grad, cross_send, cross_recv, g_send, g_recv = [refs.pop(0) for _ in range(6)]
     me = lax.axis_index("seq")
     phase = lax.axis_index("phase")
     barrier = pltpu.get_barrier_semaphore()
-    y_copy = pltpu.make_async_remote_copy(
-        src_ref=y_ref, dst_ref=x_ref, send_sem=y_send, recv_sem=y_recv,
-        device_id={"phase": 1 - phase, "seq": me}, device_id_type=MESH,
-    )
-
-    def copy(k, slot):
-        return pltpu.make_async_remote_copy(
-            src_ref=part, dst_ref=held.at[slot], send_sem=send_sem.at[k], recv_sem=recv_sem.at[slot],
-            device_id={"phase": 1 - phase, "seq": lax.rem(me + k, n)}, device_id_type=MESH,
+
+    def other(k):
+        return lax.rem(me + k, n)
+
+    def greet(section, start):
+        def signal(k, _):
+            pl.semaphore_signal(
+                barrier, inc=1, device_id={"phase": section, "seq": other(k)}, device_id_type=MESH
+            )
+            return 0
+
+        lax.fori_loop(start, n, signal, 0)
+
+    if ahead:
+        y_copy = pltpu.make_async_remote_copy(
+            src_ref=y_ref, dst_ref=x_out, send_sem=y_send, recv_sem=y_recv,
+            device_id={"phase": 1 - phase, "seq": me}, device_id_type=MESH,
         )
+
+        def square_copy(k, slot):
+            return pltpu.make_async_remote_copy(
+                src_ref=square, dst_ref=held.at[slot], send_sem=send_sem.at[k], recv_sem=recv_sem.at[slot],
+                device_id={"phase": 1 - phase, "seq": other(k)}, device_id_type=MESH,
+            )
+
+    if back:
+        g_copy = pltpu.make_async_remote_copy(
+            src_ref=grad, dst_ref=g_out, send_sem=g_send, recv_sem=g_recv,
+            device_id={"phase": 1 - phase, "seq": me}, device_id_type=MESH,
+        )
+
+        def cross_copy(k, slot):
+            return pltpu.make_async_remote_copy(
+                src_ref=cross_ref, dst_ref=crosses.at[slot], send_sem=cross_send.at[k],
+                recv_sem=cross_recv.at[slot],
+                device_id={"phase": phase, "seq": other(k)}, device_id_type=MESH,
+            )
 
     @pl.when(phase == 1)
     def _():
-        def greet(k, _):
-            pl.semaphore_signal(
-                barrier, inc=1, device_id={"phase": 0, "seq": lax.rem(me + k, n)}, device_id_type=MESH
-            )
-            return 0
-
-        lax.fori_loop(0, n, greet, 0)
-
-        def take(k, total):
-            source = lax.rem(me + k, n)
-            copy(k, source).wait_recv()
-            return total + held[source]
-
-        total_ref[...] = lax.fori_loop(0, n, take, jnp.zeros(total_ref.shape, jnp.float32))
-        y_copy.wait_recv()
+        if back:
+            greet(1, 1)
+        if ahead:
+            greet(0, 0)
+        if back:
+            pl.semaphore_wait(barrier, n)
+
+            def send(k, _):
+                cross_copy(k, me).start()
+                return 0
+
+            lax.fori_loop(1, n, send, 0)
+
+            def take(k, total):
+                cross_copy(k, other(k)).wait_recv()
+                return total + crosses[other(k)]
+
+            cross = lax.fori_loop(1, n, take, cross_ref[...])
+            inv = lax.rsqrt(total_ref[...] / width + eps)
+            factor = inv * inv * inv * (cross / width)
+            grad[...] = (part_ref[...] - x_ref[...].astype(jnp.float32) * factor).astype(jnp.bfloat16)
+            g_copy.start()
+        if ahead:
+            def take_square(k, total):
+                square_copy(k, other(k)).wait_recv()
+                return total + held[other(k)]
+
+            total_out[...] = lax.fori_loop(0, n, take_square, jnp.zeros(total_out.shape, jnp.float32))
+            y_copy.wait_recv()
+        if back:
+            def finish(k, _):
+                cross_copy(k, me).wait_send()
+                return 0
+
+            lax.fori_loop(1, n, finish, 0)
+            g_copy.wait_send()
 
     @pl.when(phase == 0)
     def _():
-        yf = y_ref[...].astype(jnp.float32)
-        part[...] = jnp.sum(yf * yf, axis=0, keepdims=True)
-        pl.semaphore_wait(barrier, n)
-        y_copy.start()
-
-        def send(k, _):
-            copy(k, me).start()
-            return 0
-
-        lax.fori_loop(0, n, send, 0)
-
-        def finish(k, _):
-            copy(k, me).wait_send()
-            return 0
-
-        lax.fori_loop(0, n, finish, 0)
-        y_copy.wait_send()
-
-
-def ahead(n, y):
+        if back:
+            pl.semaphore_signal(barrier, inc=1, device_id={"phase": 1, "seq": me}, device_id_type=MESH)
+        if ahead:
+            yf = y_ref[...].astype(jnp.float32)
+            square[...] = jnp.sum(yf * yf, axis=0, keepdims=True)
+            pl.semaphore_wait(barrier, n)
+
+            def send(k, _):
+                square_copy(k, me).start()
+                return 0
+
+            lax.fori_loop(0, n, send, 0)
+            y_copy.start()
+        if back:
+            g_copy.wait_recv()
+        if ahead:
+            def finish(k, _):
+                square_copy(k, me).wait_send()
+                return 0
+
+            lax.fori_loop(0, n, finish, 0)
+            y_copy.wait_send()
+
+
+def exchange(n, width, y=None, back=None):
     vmem = pl.BlockSpec(memory_space=pltpu.VMEM)
-    rows = y.shape[1]
+    ahead = y is not None
+    operands, shapes, scratch = [], [], []
+    feats, rows = y.shape if ahead else back[0].shape
+    whole = jax.ShapeDtypeStruct((feats, rows), jnp.bfloat16)
+    row = jax.ShapeDtypeStruct((1, rows), jnp.float32)
+    sems = [pltpu.SemaphoreType.DMA((n,)), pltpu.SemaphoreType.DMA((n,)), pltpu.SemaphoreType.DMA, pltpu.SemaphoreType.DMA]
+    if ahead:
+        operands.append(y)
+        shapes += [whole, row]
+        scratch += [pltpu.VMEM((1, rows), jnp.float32), pltpu.VMEM((n, 1, rows), jnp.float32)] + sems
+    if back is not None:
+        operands += list(back)
+        shapes.append(whole)
+        scratch += [pltpu.VMEM((n, 1, rows), jnp.float32), pltpu.VMEM((feats, rows), jnp.bfloat16)] + sems
     return pl.pallas_call(
-        functools.partial(ahead_kernel, n),
-        out_shape=[jax.ShapeDtypeStruct(y.shape, y.dtype), jax.ShapeDtypeStruct((1, rows), jnp.float32)],
-        in_specs=[vmem],
-        out_specs=[vmem, vmem],
-        scratch_shapes=[
-            pltpu.VMEM((1, rows), jnp.float32),
-            pltpu.VMEM((n, 1, rows), jnp.float32),
-            pltpu.SemaphoreType.DMA((n,)),
-            pltpu.SemaphoreType.DMA((n,)),
-            pltpu.SemaphoreType.DMA,
-            pltpu.SemaphoreType.DMA,
-        ],
-        compiler_params=pltpu.CompilerParams(collective_id=1, has_side_effects=True),
-        name="relay_ahead",
-    )(y)
-
-
-def back_kernel(n, width, part_ref, cross_ref, x_ref, total_ref, g_ref, held, grad, send_sem, recv_sem, g_send, g_recv):
-    me = lax.axis_index("seq")
-    phase = lax.axis_index("phase")
-    barrier = pltpu.get_barrier_semaphore()
-    g_copy = pltpu.make_async_remote_copy(
-        src_ref=grad, dst_ref=g_ref, send_sem=g_send, recv_sem=g_recv,
-        device_id={"phase": 1 - phase, "seq": me}, device_id_type=MESH,
-    )
-
-    def copy(k, slot):
-        return pltpu.make_async_remote_copy(
-            src_ref=cross_ref, dst_ref=held.at[slot], send_sem=send_sem.at[k], recv_sem=recv_sem.at[slot],
-            device_id={"phase": phase, "seq": lax.rem(me + k, n)}, device_id_type=MESH,
-        )
-
-    @pl.when(phase == 0)
-    def _():
-        pl.semaphore_signal(barrier, inc=1, device_id={"phase": 1, "seq": me}, device_id_type=MESH)
-        g_copy.wait_recv()
-
-    @pl.when(phase == 1)
-    def _():
-        def greet(k, _):
-            pl.semaphore_signal(
-                barrier, inc=1, device_id={"phase": 1, "seq": lax.rem(me + k, n)}, device_id_type=MESH
-            )
-            return 0
-
-        lax.fori_loop(1, n, greet, 0)
-        pl.semaphore_wait(barrier, n)
-
-        def send(k, _):
-            copy(k, me).start()
-            return 0
-
-        lax.fori_loop(1, n, send, 0)
-
-        def take(k, total):
-            source = lax.rem(me + k, n)
-            copy(k, source).wait_recv()
-            return total + held[source]
-
-        cross = lax.fori_loop(1, n, take, cross_ref[...])
-        inv = lax.rsqrt(total_ref[...] / width + eps)
-        factor = inv * inv * inv * (cross / width)
-        grad[...] = (part_ref[...] - x_ref[...].astype(jnp.float32) * factor).astype(jnp.bfloat16)
-        g_copy.start()
-
-        def finish(k, _):
-            copy(k, me).wait_send()
-            return 0
-
-        lax.fori_loop(1, n, finish, 0)
-        g_copy.wait_send()
-
-
-def back(n, width, part, cross, x, total):
-    vmem = pl.BlockSpec(memory_space=pltpu.VMEM)
-    rows = x.shape[1]
+        functools.partial(exchange_kernel, n, width, ahead, back is not None),
+        out_shape=shapes,
+        in_specs=[vmem] * len(operands),
+        out_specs=[vmem] * len(shapes),
+        scratch_shapes=scratch,
+        compiler_params=pltpu.CompilerParams(
+            collective_id=int(ahead) + 2 * int(back is not None), has_side_effects=True
+        ),
+        name="exchange" + ("_ahead" if ahead else "") + ("_back" if back is not None else ""),
+    )(*operands)
+
+
+def scatter_kernel(m, kv_ref, out_ref, sems):
+    n, _, columns = out_ref.shape
+    copies = [
+        pltpu.make_async_copy(kv_ref.at[0, m, :, pl.ds(j * columns, columns)], out_ref.at[j], sems.at[j])
+        for j in range(n)
+    ]
+    for copy in copies:
+        copy.start()
+    for copy in copies:
+        copy.wait()
+
+
+def scatter(n, m, enc_kv):
+    _, _, rows, columns = enc_kv.shape
+    spec = pl.BlockSpec(memory_space=pl.ANY)
     return pl.pallas_call(
-        functools.partial(back_kernel, n, width),
-        out_shape=jax.ShapeDtypeStruct(x.shape, jnp.bfloat16),
-        in_specs=[vmem] * 4,
-        out_specs=vmem,
-        scratch_shapes=[
-            pltpu.VMEM((n, 1, rows), jnp.float32),
-            pltpu.VMEM(x.shape, jnp.bfloat16),
-            pltpu.SemaphoreType.DMA((n,)),
-            pltpu.SemaphoreType.DMA((n,)),
-            pltpu.SemaphoreType.DMA,
-            pltpu.SemaphoreType.DMA,
-        ],
-        compiler_params=pltpu.CompilerParams(collective_id=2, has_side_effects=True),
-        name="relay_back",
-    )(part, cross, x, total)
+        functools.partial(scatter_kernel, m),
+        out_shape=jax.ShapeDtypeStruct((n, rows, columns // n), enc_kv.dtype),
+        in_specs=[spec],
+        out_specs=spec,
+        scratch_shapes=[pltpu.SemaphoreType.DMA((n,))],
+        name="scatter",
+    )(enc_kv)
+
+
+def gather_kernel(*refs):
+    *parts, out_ref, sems = refs
+    n, _, columns = parts[0].shape
+    copies = [
+        pltpu.make_async_copy(part.at[j], out_ref.at[0, m, :, pl.ds(j * columns, columns)], sems.at[m * n + j])
+        for m, part in enumerate(parts) for j in range(n)
+    ]
+    for copy in copies:
+        copy.start()
+    for copy in copies:
+        copy.wait()
+
+
+def gather(parts):
+    n, rows, columns = parts[0].shape
+    spec = pl.BlockSpec(memory_space=pl.ANY)
+    return pl.pallas_call(
+        gather_kernel,
+        out_shape=jax.ShapeDtypeStruct((1, len(parts), rows, n * columns), parts[0].dtype),
+        in_specs=[spec] * len(parts),
+        out_specs=spec,
+        scratch_shapes=[pltpu.SemaphoreType.DMA((n * len(parts),))],
+        name="gather",
+    )(*parts)
 
 
 def doc_bounds(qseg, kseg):
@@ -441,9 +486,11 @@
     first_totals = totals(n, jnp.sum(xf * xf, axis=1))
     scattered = []
     for m in range(micro):
-        blocks = enc_kv[0, m].reshape(own_enc, n, 2 * feats).transpose(1, 0, 2)
+        blocks = scatter(n, m, enc_kv)
         if m > 0:
-            blocks, scattered[-1], first_totals = lax.optimization_barrier((blocks, scattered[-1], first_totals))
+            blocks, scattered[-1] = lax.optimization_barrier((blocks, scattered[-1]))
+        else:
+            blocks, first_totals = lax.optimization_barrier((blocks, first_totals))
         scattered.append(lax.all_to_all(blocks, "seq", split_axis=0, concat_axis=0, tiled=True))
 
     calls, x0s, t0s = [], [], []
@@ -466,35 +513,29 @@
         gogs.append(jnp.where(phase == 0, gog0, gog1))
 
     y0 = calls[0](False, 0, x=x0s[0], total=t0s[0])[0]
+    x1, total1 = exchange(n, width, y=y0)
     waiting = None
     for m in range(micro):
-        x1, total1 = ahead(n, y0)
-        if waiting is not None:
-            x1, waiting[2] = lax.optimization_barrier((x1, waiting[2]))
         y1, gkv1, part, cross, gqg1, gog1 = calls[m](True, 1, x=x1, total=total1, g=wanted[m])
         if waiting is not None:
             waiting[2], part = lax.optimization_barrier((waiting[2], part))
             finish(m - 1, *waiting)
-        later = None
+        waiting = [y0, (y1, gkv1, gqg1, gog1), None]
         if m + 1 < micro:
             x_next, part = lax.optimization_barrier((x0s[m + 1], part))
-            later = calls[m + 1](False, 0, x=x_next, total=t0s[m + 1])[0]
-            cross, later = lax.optimization_barrier((cross, later))
-        g0 = back(n, width, part, cross, x1, total1)
-        if grads:
-            grads[-1], g0 = lax.optimization_barrier((grads[-1], g0))
-        if later is not None:
-            later, g0 = lax.optimization_barrier((later, g0))
-        waiting = [y0, (y1, gkv1, gqg1, gog1), g0]
-        y0 = later
+            y0 = calls[m + 1](False, 0, x=x_next, total=t0s[m + 1])[0]
+            x1, total1, waiting[2] = exchange(n, width, y=y0, back=(part, cross, x1, total1))
+        else:
+            waiting[2] = exchange(n, width, back=(part, cross, x1, total1))[0]
+            if grads:
+                grads[-1], waiting[2] = lax.optimization_barrier((grads[-1], waiting[2]))
     finish(micro - 1, *waiting)
     returned = []
     for m in range(micro):
-        rows_back = lax.all_to_all(grads[m], "seq", split_axis=0, concat_axis=0, tiled=True)
-        returned.append(rows_back.transpose(1, 0, 2).reshape(own_enc, 2 * feats * n))
+        returned.append(lax.all_to_all(grads[m], "seq", split_axis=0, concat_axis=0, tiled=True))
     return (
         jnp.stack(outs)[None],
-        jnp.stack(returned)[None],
+        gather(returned),
         sum(gqgs).reshape(1, feats),
         sum(gogs).reshape(1, feats),
     )

time: 364 us -> 564 us (1.55); the launches traced: 364 us -> 556 us
  Pallas kernels: 206 us -> 394 us
  waiting for transfers between devices: 35.6 us -> 44.9 us
  other arithmetic: 12.6 us -> 6.14 us
    pallas_call x4 -> x6, Pallas kernels: 76.7 us -> 328 us  [the longest x2 130 us: scatter(): pl.pallas_call(functools.partial(scatter_kernel, m), out_shape=jax.ShapeD...]
    pallas_call x1, Pallas kernels: 49.2 us -> 8.58 us  [totals(): pl.pallas_call(functools.partial(totals_kernel, n), out_shape=jax.ShapeDt...]
    unnamed x47 -> x135, local copies, waits for them, and re-layouts: 5.91 us -> 31.6 us
    pallas_call x6, Pallas kernels: 80.5 us -> 57.3 us  [attention(): pl.pallas_call(functools.partial(attention_kernel, backward, active, widt...]
    another operation x4 -> x0, local copies, waits for them, and re-layouts: 13.6 us -> none  [the longest x2 8.6 us: local(): jnp.stack(returned)[None]]
    all_to_all x1, waiting for transfers between devices: 35.5 us -> 44.9 us  [local(): lax.all_to_all(grads[m], 'seq', split_axis=0, concat_axis=0, tiled=True)]
    transpose x2 -> x0, local copies, waits for them, and re-layouts: 6.55 us -> none  [local(): rows_back.transpose(1, 0, 2).reshape(own_enc, 2 * feats * n)]
  transfers between devices with their start and end apart: 3 -> 3, of which waited for: 1 -> 1; matrix products, arithmetic and copies ran while one was open for 7% -> 2% of each run, Pallas kernels for 24% -> 18%
where the time goes in v2:
time: 564 us; the launch traced here: 556 us
  Pallas kernels  394 us (70%)
  blocking collectives  53.7 us (10%)
  waiting for transfers between devices  44.9 us (8%)
  local copies, waits for them, and re-layouts  38.4 us (7%)
  starting transfers between devices  17.9 us (3%)
  other arithmetic  6.14 us (1%)
    pallas_call x2, Pallas kernels, scatter(): pl.pallas_call(functools.partial(scatter_kernel, m), out_shape=jax.ShapeD...  130 us
    pallas_call x1, Pallas kernels, gather(): pl.pallas_call(gather_kernel, out_shape=jax.ShapeDtypeStruct((1, len(part...  128 us
    pallas_call x3, Pallas kernels, exchange(): pl.pallas_call(functools.partial(exchange_kernel, n, width, ahead, back i...  70 us
    pallas_call x6, Pallas kernels, attention(): pl.pallas_call(functools.partial(attention_kernel, backward, active, widt...  57.3 us
    all_to_all x1, blocking collectives, local(): lax.all_to_all(grads[m], 'seq', split_axis=0, concat_axis=0, tiled=True)  53.7 us
    all_to_all x1, waiting for transfers between devices, local(): lax.all_to_all(grads[m], 'seq', split_axis=0, concat_axis=0, tiled=True)  44.9 us
    unnamed x135, local copies, waits for them, and re-layouts  31.6 us
    all_to_all x2, starting transfers between devices, local(): lax.all_to_all(blocks, 'seq', split_axis=0, concat_axis=0, tiled=True)  12.6 us
  transfers between devices with their start and end apart: 3, of which 1 were waited for; matrix products, arithmetic and copies ran while one was open for 2% of the time, Pallas kernels for 18%

profile of v2, /device:TPU:13, one launch (start us, length us, event | category | flops | bytes accessed | tf_op | source)
XLA Modules:
  0.0 556.3 jit_solution(10843827831527126859)
XLA Ops:
  2.7 8.6 %row_totals.1 = f32[2,512]{1,0:T(2,128)} custom-call(f32[2,512]{1,0:T(2,128)} %multiply_reduce_fusion.part_ref), custom_call_target="tpu_custom_call" | custom-call | tf_op jit(solution)/shard_map/row_totals/pallas_call | solution.py:254
  11.2 64.8 %scatter.3 = bf16[16,128,512]{2,1,0:T(8,128)(2,1)} custom-call(bf16[1,2,128,8192]{3,2,1,0:T(8,128)(2,1)} %kv_ref.3), custom_call_target="tpu_custom_call" | custom-call | tf_op jit(solution)/shard_map/scatter/pallas_call | solution.py:429
  76.0 6.5 %all-to-all-start = ((bf16[16,128,512]{2,1,0:T(8,128)(2,1)}), bf16[16,128,512]{2,1,0:T(8,128)(2,1)S(1)}, u32[]{:S(2)}, u32[]{:S(2)}) async-start(bf16[16,128,512]{2,1,0:T(8,128)(2,1)} %scatter.3), calls=%async_computation | async-start | bytes 4194304 | tf_op jit(solution)/shard_map/all_to_all | solution.py:494
  82.5 64.8 %scatter.2 = bf16[16,128,512]{2,1,0:T(8,128)(2,1)} custom-call(bf16[1,2,128,8192]{3,2,1,0:T(8,128)(2,1)} %kv_ref.3), custom_call_target="tpu_custom_call" | custom-call | tf_op jit(solution)/shard_map/scatter/pallas_call | solution.py:429
  148.0 6.2 %all-to-all-start.1 = ((bf16[16,128,512]{2,1,0:T(8,128)(2,1)}), bf16[16,128,512]{2,1,0:T(8,128)(2,1)}, u32[]{:S(2)}, u32[]{:S(2)}) async-start(bf16[16,128,512]{2,1,0:T(8,128)(2,1)} %scatter.2), calls=%async_computation.1 | async-start | bytes 4194304 | tf_op jit(solution)/shard_map/all_to_all | solution.py:494
  156.9 1.4 copy.51.refs_3_
  158.6 2.0 slice_bitcast_fusion
  160.6 1.8 slice_bitcast_fusion.3
  162.4 9.5 %section_ahead.2.refs_0_ = bf16[256,512]{1,0:T(8,128)(2,1)S(1)} custom-call(s32[1]{0:T(128)} %bitcast.refs_0_, s32[4]{0:T(128)S(1)} %reshape.248.refs_1_, bf16[2048,512]{1,0:T(8,128)(2,1)S(1)} %bitcast.72, s32[2048,1]{1,0:T(8,128)S(1)} %copy-done.6, s32[1,512]{1,0:T(1,128)S(1)} %get-tuple-element.98.refs_4_, bf16[256,512]{1,0:T(8,128)(2,1)S(1)} %get-tuple-element.90.refs_5_, ...), custom_call_target="tpu_custom_call" | custom-call | flops 8589934592 | bytes 4194304 | tf_op jit(solution)/shard_map/section_ahead/pallas_call | solution.py:200
  173.4 27.8 %exchange_ahead.1 = (bf16[256,512]{1,0:T(8,128)(2,1)}, f32[1,512]{1,0:T(1,128)}) custom-call(bf16[256,512]{1,0:T(8,128)(2,1)} %copy-done.9), custom_call_target="tpu_custom_call" | custom-call | tf_op jit(solution)/shard_map/exchange_ahead/pallas_call | solution.py:401
  201.1 1.6 copy-done.4
  214.9 9.8 %section_ahead.3.refs_0_ = bf16[256,512]{1,0:T(8,128)(2,1)S(1)} custom-call(s32[1]{0:T(128)} %bitcast.refs_0_, s32[4]{0:T(128)S(1)} %copy-done.51, bf16[2048,512]{1,0:T(8,128)(2,1)} %bitcast.21.refs_2_, s32[2048,1]{1,0:T(8,128)S(1)} %copy.61.refs_3_, s32[1,512]{1,0:T(1,128)S(1)} %get-tuple-element.99.refs_4_, bf16[256,512]{1,0:T(8,128)(2,1)S(1)} %copy-done.15, ...), custom_call_target="tpu_custom_call" | custom-call | flops 8589934592 | bytes 4194304 | tf_op jit(solution)/shard_map/section_ahead/pallas_call | solution.py:200
  225.4 27.4 %exchange_ahead_back.1 = (bf16[256,512]{1,0:T(8,128)(2,1)}, f32[1,512]{1,0:T(1,128)}, bf16[256,512]{1,0:T(8,128)(2,1)}) custom-call(bf16[256,512]{1,0:T(8,128)(2,1)} %copy-done.11, f32[256,512]{1,0:T(8,128)} %copy-done.14, f32[1,512]{1,0:T(1,128)} %copy-done.49, bf16[256,512]{1,0:T(8,128)(2,1)} %get-tuple-element.40.refs_5_.refs_3_, ...), custom_call_target="tpu_custom_call" | custom-call | tf_op jit(solution)/shard_map/exchange_ahead_back/pallas_call | solution.py:401
  257.9 1.9 section_back.5
  259.8 1.4 copy-done
  264.7 18.0 %section_back.6 = (bf16[256,512]{1,0:T(8,128)(2,1)}, bf16[2048,512]{1,0:T(8,128)(2,1)S(1)}, f32[256,512]{1,0:T(8,128)}, f32[1,512]{1,0:T(1,128)}, f32[256,1]{1,0:T(8,128)S(1)}, /*index=5*/f32[256,1]{1,0:T(8,128)S(1)}) custom-call(s32[1]{0:T(128)} %bitcast.refs_0_, s32[4]{0:T(128)S(1)} %copy-done.56, bf16[2048,512]{1,0:T(8,128)(2,1)S(1)} %bitcast.74, ...), custom_call_target="tpu_custom_call" | custom-call | flops 19327352832 | bytes 4194304 | tf_op jit(solution)/shard_map/section_back/pallas_call | solution.py:200
  282.7 1.3 copy-done.2
  285.3 14.9 %exchange_back.1.refs_9_ = bf16[256,512]{1,0:T(8,128)(2,1)} custom-call(f32[256,512]{1,0:T(8,128)} %copy-done.13, f32[1,512]{1,0:T(1,128)} %copy-done.47, bf16[256,512]{1,0:T(8,128)(2,1)} %get-tuple-element.48.refs_5_.refs_2_, f32[1,512]{1,0:T(1,128)} %get-tuple-element.49.refs_6_.refs_3_), custom_call_target="tpu_custom_call" | custom-call | tf_op jit(solution)/shard_map/exchange_back/pallas_call | solution.py:401
  300.2 3.2 broadcast_select_fusion.1
  303.4 17.6 %section_back.7 = (bf16[256,512]{1,0:T(8,128)(2,1)}, bf16[2048,512]{1,0:T(8,128)(2,1)S(1)}, f32[256,512]{1,0:T(8,128)}, f32[1,512]{1,0:T(1,128)}, f32[256,1]{1,0:T(8,128)S(1)}, /*index=5*/f32[256,1]{1,0:T(8,128)S(1)}) custom-call(s32[1]{0:T(128)} %bitcast.refs_0_, s32[4]{0:T(128)S(1)} %copy-done.53, bf16[2048,512]{1,0:T(8,128)(2,1)} %bitcast.21.refs_2_, ...), custom_call_target="tpu_custom_call" | custom-call | flops 19327352832 | bytes 4194304 | tf_op jit(solution)/shard_map/section_back/pallas_call | solution.py:200
  321.2 53.7 %all_to_all.20.refs_1_ = bf16[16,128,512]{2,1,0:T(8,128)(2,1)} all-to-all(bf16[16,128,512]{2,1,0:T(8,128)(2,1)S(1)} %bitcast.76), channel_id=1, replica_groups=mesh['phase'=2,'seq'=16] {'seq'}, dimensions={0} | all-to-all | bytes 4194304 | tf_op jit(solution)/shard_map/all_to_all | solution.py:535
  374.9 5.3 all-to-all-start.2
  382.7 44.9 %all-to-all-done.2.refs_0_ = bf16[16,128,512]{2,1,0:T(8,128)(2,1)} async-done(((bf16[16,128,512]{2,1,0:T(8,128)(2,1)}), bf16[16,128,512]{2,1,0:T(8,128)(2,1)}, u32[]{:S(2)}, u32[]{:S(2)}) %all-to-all-start.2) | async-done | bytes 2097184 | tf_op jit(solution)/shard_map/all_to_all | solution.py:535
  427.7 128.4 %gather.1 = bf16[1,2,128,8192]{3,2,1,0:T(8,128)(2,1)} custom-call(bf16[16,128,512]{2,1,0:T(8,128)(2,1)} %all-to-all-done.2.refs_0_, bf16[16,128,512]{2,1,0:T(8,128)(2,1)} %all_to_all.20.refs_1_), custom_call_target="tpu_custom_call" | custom-call | tf_op jit(solution)/shard_map/gather/pallas_call | solution.py:455
  (162 shorter events, 32.5 us)
Async XLA Ops:
  1.9 74.1 %copy-start.57 = (bf16[2,512,256]{1,2,0:T(8,128)(2,1)}, bf16[2,512,256]{1,2,0:T(8,128)(2,1)S(1)}, u32[]{:S(2)}) copy-start(bf16[2,512,256]{1,2,0:T(8,128)(2,1)S(1)} %copy.50) | copy-start | bytes 1572868
  76.0 72.0 %all-to-all-start = ((bf16[16,128,512]{2,1,0:T(8,128)(2,1)}), bf16[16,128,512]{2,1,0:T(8,128)(2,1)S(1)}, u32[]{:S(2)}, u32[]{:S(2)}) async-start(bf16[16,128,512]{2,1,0:T(8,128)(2,1)} %scatter.3), calls=%async_computation | async-start | bytes 4194304 | tf_op jit(solution)/shard_map/all_to_all | solution.py:494
  82.5 64.8 %copy-start.61 = (s32[2,512]{1,0:T(2,128)S(1)}, s32[2,512]{1,0:T(2,128)}, u32[]{:S(2)}) copy-start(s32[2,512]{1,0:T(2,128)} %param.9) | copy-start | bytes 12292
  82.5 65.1 %copy-start.59 = (s32[2,2048]{1,0:T(2,128)S(1)}, s32[2,2048]{1,0:T(2,128)}, u32[]{:S(2)}) copy-start(s32[2,2048]{1,0:T(2,128)} %param.10) | copy-start | bytes 49156
  148.0 7.6 %copy-start.62 = (f32[1,256]{1,0:T(1,128)S(1)}, f32[1,256]{1,0:T(1,128)}, u32[]{:S(2)}) copy-start(f32[1,256]{1,0:T(1,128)} %param.11) | copy-start | bytes 3076
  148.0 7.7 %copy-start.63 = (f32[1,256]{1,0:T(1,128)S(1)}, f32[1,256]{1,0:T(1,128)}, u32[]{:S(2)}) copy-start(f32[1,256]{1,0:T(1,128)} %param.12) | copy-start | bytes 3076
  148.0 7.9 %copy-start.58 = (bf16[2,512,256]{2,1,0:T(8,128)(2,1)S(1)}, bf16[2,512,256]{2,1,0:T(8,128)(2,1)}, u32[]{:S(2)}) copy-start(bf16[2,512,256]{2,1,0:T(8,128)(2,1)} %param.13) | copy-start | bytes 1572868
  148.0 14.4 %copy-start.3 = (bf16[16,128,512]{2,1,0:T(8,128)(2,1)}, bf16[16,128,512]{2,1,0:T(8,128)(2,1)S(1)}, u32[]{:S(2)}) copy-start(bf16[16,128,512]{2,1,0:T(8,128)(2,1)S(1)} %all-to-all-done) | copy-start | bytes 6291460
  148.0 63.5 %all-to-all-start.1 = ((bf16[16,128,512]{2,1,0:T(8,128)(2,1)}), bf16[16,128,512]{2,1,0:T(8,128)(2,1)}, u32[]{:S(2)}, u32[]{:S(2)}) async-start(bf16[16,128,512]{2,1,0:T(8,128)(2,1)} %scatter.2), calls=%async_computation.1 | async-start | bytes 4194304 | tf_op jit(solution)/shard_map/all_to_all | solution.py:494
  154.2 4.4 copy-start.60
  155.5 6.9 %copy-start.54 = (s32[4]{0:T(128)}, s32[4]{0:T(128)S(1)}, u32[]{:S(2)}) copy-start(s32[4]{0:T(128)S(1)} %reshape.248.refs_1_) | copy-start | bytes 52
  155.7 6.7 %copy-start.36 = (f32[256,1]{1,0:T(8,128)}, f32[256,1]{1,0:T(8,128)S(1)}, u32[]{:S(2)}) copy-start(f32[256,1]{1,0:T(8,128)S(1)} %copy.52.refs_7_) | copy-start | bytes 3076
  155.8 6.5 %copy-start.41 = (f32[256,1]{1,0:T(8,128)}, f32[256,1]{1,0:T(8,128)S(1)}, u32[]{:S(2)}) copy-start(f32[256,1]{1,0:T(8,128)S(1)} %copy.53.refs_8_) | copy-start | bytes 3076
  158.6 3.8 copy-start.6
  257.9 6.8 %copy-start.5 = (bf16[16,128,512]{2,1,0:T(8,128)(2,1)S(1)}, bf16[16,128,512]{2,1,0:T(8,128)(2,1)}, u32[]{:S(2)}) copy-start(bf16[16,128,512]{2,1,0:T(8,128)(2,1)} %copy-done.3) | copy-start | bytes 6291460
  257.9 6.8 %copy-start.8 = (s32[2048,1]{1,0:T(8,128)S(1)}, s32[2048,1]{1,0:T(8,128)}, u32[]{:S(2)}) copy-start(s32[2048,1]{1,0:T(8,128)} %copy.51.refs_3_) | copy-start | bytes 24580
  257.9 6.8 %copy-start.20 = (bf16[256,512]{1,0:T(8,128)(2,1)S(1)}, bf16[256,512]{1,0:T(8,128)(2,1)}, u32[]{:S(2)}) copy-start(bf16[256,512]{1,0:T(8,128)(2,1)} %copy-done.19) | copy-start | bytes 786436
  257.9 6.8 %copy-start.50 = (bf16[256,512]{1,0:T(8,128)(2,1)S(1)}, bf16[256,512]{1,0:T(8,128)(2,1)}, u32[]{:S(2)}) copy-start(bf16[256,512]{1,0:T(8,128)(2,1)} %get-tuple-element.53.refs_9_) | copy-start | bytes 786436
  257.9 6.8 %copy-start.56 = (s32[4]{0:T(128)S(1)}, s32[4]{0:T(128)}, u32[]{:S(2)}) copy-start(s32[4]{0:T(128)} %copy-done.54) | copy-start | bytes 52
  303.4 17.6 %copy-start.1 = (bf16[2048,512]{1,0:T(8,128)(2,1)S(1)}, bf16[2048,512]{1,0:T(8,128)(2,1)}, u32[]{:S(2)}) copy-start(bf16[2048,512]{1,0:T(8,128)(2,1)} %copy-done) | copy-start | bytes 6291460
  374.9 5.3 copy-start.10
  374.9 5.4 copy-start.12
  374.9 5.4 copy-start.18
  374.9 52.8 %all-to-all-start.2 = ((bf16[16,128,512]{2,1,0:T(8,128)(2,1)}), bf16[16,128,512]{2,1,0:T(8,128)(2,1)}, u32[]{:S(2)}, u32[]{:S(2)}) async-start(bf16[16,128,512]{2,1,0:T(8,128)(2,1)} %bitcast.75), calls=%async_computation.2 | async-start | bytes 4194304 | tf_op jit(solution)/shard_map/all_to_all | solution.py:535
  (43 other events, 51.4 us)

commit v3 on v2

--- a/solution.py
+++ b/solution.py
@@ -15,7 +15,7 @@
 eps = 1e-06
 neg_big = -1e30
 MESH = pl.DeviceIdType.MESH
-VMEM_BYTES = 36 * 1024 * 1024
+VMEM_BYTES = 56 * 1024 * 1024
 
 
 def matmul(a, b):
@@ -411,53 +411,43 @@
     )(*operands)
 
 
-def scatter_kernel(m, kv_ref, out_ref, sems):
+def scatter_kernel(kv_ref, out_ref):
     n, _, columns = out_ref.shape
-    copies = [
-        pltpu.make_async_copy(kv_ref.at[0, m, :, pl.ds(j * columns, columns)], out_ref.at[j], sems.at[j])
-        for j in range(n)
-    ]
-    for copy in copies:
-        copy.start()
-    for copy in copies:
-        copy.wait()
+    for j in range(n):
+        out_ref[j] = kv_ref[0, 0, :, j * columns:(j + 1) * columns]
 
 
 def scatter(n, m, enc_kv):
     _, _, rows, columns = enc_kv.shape
-    spec = pl.BlockSpec(memory_space=pl.ANY)
     return pl.pallas_call(
-        functools.partial(scatter_kernel, m),
+        scatter_kernel,
+        grid=(1,),
         out_shape=jax.ShapeDtypeStruct((n, rows, columns // n), enc_kv.dtype),
-        in_specs=[spec],
-        out_specs=spec,
-        scratch_shapes=[pltpu.SemaphoreType.DMA((n,))],
+        in_specs=[pl.BlockSpec((1, 1, rows, columns), lambda i: (0, m, 0, 0))],
+        out_specs=pl.BlockSpec((n, rows, columns // n), lambda i: (0, 0, 0)),
+        compiler_params=pltpu.CompilerParams(vmem_limit_bytes=VMEM_BYTES),
         name="scatter",
     )(enc_kv)
 
 
 def gather_kernel(*refs):
-    *parts, out_ref, sems = refs
+    *parts, out_ref = refs
     n, _, columns = parts[0].shape
-    copies = [
-        pltpu.make_async_copy(part.at[j], out_ref.at[0, m, :, pl.ds(j * columns, columns)], sems.at[m * n + j])
-        for m, part in enumerate(parts) for j in range(n)
-    ]
-    for copy in copies:
-        copy.start()
-    for copy in copies:
-        copy.wait()
+    for m, part in enumerate(parts):
+        for j in range(n):
+            out_ref[0, m, :, j * columns:(j + 1) * columns] = part[j]
 
 
 def gather(parts):
     n, rows, columns = parts[0].shape
-    spec = pl.BlockSpec(memory_space=pl.ANY)
+    tile = 32 if rows % 32 == 0 else rows
     return pl.pallas_call(
         gather_kernel,
+        grid=(rows // tile,),
         out_shape=jax.ShapeDtypeStruct((1, len(parts), rows, n * columns), parts[0].dtype),
-        in_specs=[spec] * len(parts),
-        out_specs=spec,
-        scratch_shapes=[pltpu.SemaphoreType.DMA((n * len(parts),))],
+        in_specs=[pl.BlockSpec((n, tile, columns), lambda i: (0, i, 0))] * len(parts),
+        out_specs=pl.BlockSpec((1, len(parts), tile, n * columns), lambda i: (0, 0, i, 0)),
+        compiler_params=pltpu.CompilerParams(vmem_limit_bytes=VMEM_BYTES),
         name="gather",
     )(*parts)
 
@@ -532,7 +522,10 @@
     finish(micro - 1, *waiting)
     returned = []
     for m in range(micro):
-        returned.append(lax.all_to_all(grads[m], "seq", split_axis=0, concat_axis=0, tiled=True))
+        grad = grads[m]
+        if returned:
+            grad, returned[-1] = lax.optimization_barrier((grad, returned[-1]))
+        returned.append(lax.all_to_all(grad, "seq", split_axis=0, concat_axis=0, tiled=True))
     return (
         jnp.stack(outs)[None],
         gather(returned),

time: 564 us -> 315 us (0.56); the launches traced: 556 us -> 314 us
  Pallas kernels: 394 us -> 155 us
  waiting for transfers between devices: 44.9 us -> 113 us
  blocking collectives: 53.7 us -> 0 us
  local copies, waits for them, and re-layouts: 38.4 us -> 13.1 us
    pallas_call x3, Pallas kernels: 258 us -> 10.8 us  [the longest x2 6.13 us: scatter(): pl.pallas_call(scatter_kernel, grid=(1,), out_shape=jax.ShapeDtypeStruct(...]
    all_to_all x1 -> x0, blocking collectives: 53.7 us -> none  [local(): lax.all_to_all(grads[m], 'seq', split_axis=0, concat_axis=0, tiled=True)]
    all_to_all x2, waiting for transfers between devices: 0.01 us -> 43.1 us  [local(): lax.all_to_all(blocks, 'seq', split_axis=0, concat_axis=0, tiled=True)]
    unnamed x135 -> x51, local copies, waits for them, and re-layouts: 31.6 us -> 4.21 us
    all_to_all x1 -> x2, waiting for transfers between devices: 44.9 us -> 70.4 us  [local(): lax.all_to_all(grad, 'seq', split_axis=0, concat_axis=0, tiled=True)]
    pallas_call x6, Pallas kernels: 57.3 us -> 67.2 us  [attention(): pl.pallas_call(functools.partial(attention_kernel, backward, active, widt...]
    all_to_all x1 -> x2, starting transfers between devices: 5.25 us -> 11.4 us  [local(): lax.all_to_all(grad, 'seq', split_axis=0, concat_axis=0, tiled=True)]
  transfers between devices with their start and end apart: 3 -> 4, of which waited for: 1 -> 3; matrix products, arithmetic and copies ran while one was open for 2% -> 5% of each run, Pallas kernels for 18% -> 20%
where the time goes in v3:
time: 315 us; the launch traced here: 314 us
  Pallas kernels  155 us (49%)
  waiting for transfers between devices  113 us (36%)
  starting transfers between devices  22.7 us (7%)
  local copies, waits for them, and re-layouts  13.1 us (4%)
  other arithmetic  8.94 us (3%)
    all_to_all x2, waiting for transfers between devices, local(): lax.all_to_all(grad, 'seq', split_axis=0, concat_axis=0, tiled=True)  70.4 us
    pallas_call x3, Pallas kernels, exchange(): pl.pallas_call(functools.partial(exchange_kernel, n, width, ahead, back i...  68 us
    pallas_call x6, Pallas kernels, attention(): pl.pallas_call(functools.partial(attention_kernel, backward, active, widt...  67.2 us
    all_to_all x2, waiting for transfers between devices, local(): lax.all_to_all(blocks, 'seq', split_axis=0, concat_axis=0, tiled=True)  43.1 us
    all_to_all x2, starting transfers between devices, local(): lax.all_to_all(blocks, 'seq', split_axis=0, concat_axis=0, tiled=True)  11.4 us
    all_to_all x2, starting transfers between devices, local(): lax.all_to_all(grad, 'seq', split_axis=0, concat_axis=0, tiled=True)  11.4 us
    pallas_call x1, Pallas kernels, totals(): pl.pallas_call(functools.partial(totals_kernel, n), out_shape=jax.ShapeDt...  8.58 us
  transfers between devices with their start and end apart: 4, of which 3 were waited for; matrix products, arithmetic and copies ran while one was open for 5% of the time, Pallas kernels for 20%

profile of v3, /device:TPU:13, one launch (start us, length us, event | category | flops | bytes accessed | tf_op | source)
XLA Modules:
  0.0 313.7 jit_solution(13976683245500239679)
XLA Ops:
  2.6 8.6 %row_totals.1 = f32[2,512]{1,0:T(2,128)} custom-call(f32[2,512]{1,0:T(2,128)} %multiply_reduce_fusion.part_ref), custom_call_target="tpu_custom_call" | custom-call | tf_op jit(solution)/shard_map/row_totals/pallas_call | solution.py:254
  11.2 3.1 scatter.3
  14.3 6.5 %all-to-all-start = ((bf16[16,128,512]{2,1,0:T(8,128)(2,1)}), bf16[16,128,512]{2,1,0:T(8,128)(2,1)S(1)}, u32[]{:S(2)}, u32[]{:S(2)}) async-start(bf16[16,128,512]{2,1,0:T(8,128)(2,1)} %scatter.3), calls=%async_computation | async-start | bytes 4194304 | tf_op jit(solution)/shard_map/all_to_all | solution.py:484
  20.8 3.1 scatter.2
  25.0 43.1 %all-to-all-done = bf16[16,128,512]{2,1,0:T(8,128)(2,1)S(1)} async-done(((bf16[16,128,512]{2,1,0:T(8,128)(2,1)}), bf16[16,128,512]{2,1,0:T(8,128)(2,1)S(1)}, u32[]{:S(2)}, u32[]{:S(2)}) %all-to-all-start) | async-done | bytes 2097184 | tf_op jit(solution)/shard_map/all_to_all | solution.py:484
  68.2 4.9 %all-to-all-start.1 = ((bf16[16,128,512]{2,1,0:T(8,128)(2,1)}), bf16[16,128,512]{2,1,0:T(8,128)(2,1)}, u32[]{:S(2)}, u32[]{:S(2)}) async-start(bf16[16,128,512]{2,1,0:T(8,128)(2,1)} %scatter.2), calls=%async_computation.1 | async-start | bytes 4194304 | tf_op jit(solution)/shard_map/all_to_all | solution.py:484
  76.8 1.4 copy.51.refs_3_
  78.2 1.5 copy.61.refs_3_
  81.9 11.0 %section_ahead.2.refs_0_ = bf16[256,512]{1,0:T(8,128)(2,1)} custom-call(s32[1]{0:T(128)} %bitcast.refs_0_, s32[4]{0:T(128)} %reshape.248.refs_1_, bf16[2048,512]{1,0:T(8,128)(2,1)} %bitcast.73, s32[2048,1]{1,0:T(8,128)} %copy.51.refs_3_, s32[1,512]{1,0:T(1,128)} %get-tuple-element.102.refs_4_, bf16[256,512]{1,0:T(8,128)(2,1)} %get-tuple-element.94.refs_5_, ...), custom_call_target="tpu_custom_call" | custom-call | flops 8589934592 | bytes 4194304 | tf_op jit(solution)/shard_map/section_ahead/pallas_call | solution.py:200
  92.9 27.1 %exchange_ahead.1 = (bf16[256,512]{1,0:T(8,128)(2,1)}, f32[1,512]{1,0:T(1,128)}) custom-call(bf16[256,512]{1,0:T(8,128)(2,1)} %section_ahead.2.refs_0_), custom_call_target="tpu_custom_call" | custom-call | tf_op jit(solution)/shard_map/exchange_ahead/pallas_call | solution.py:401
  120.0 3.7 %section_back.4 = (bf16[256,512]{1,0:T(8,128)(2,1)}, bf16[2048,512]{1,0:T(8,128)(2,1)}, f32[256,512]{1,0:T(8,128)}, f32[1,512]{1,0:T(1,128)}, f32[256,1]{1,0:T(8,128)}, /*index=5*/f32[256,1]{1,0:T(8,128)}) custom-call(s32[1]{0:T(128)} %bitcast.refs_0_, s32[4]{0:T(128)} %reshape.248.refs_1_, bf16[2048,512]{1,0:T(8,128)(2,1)} %bitcast.74, ...), custom_call_target="tpu_custom_call" | custom-call | flops 19327352832 | bytes 4194304 | tf_op jit(solution)/shard_map/section_back/pallas_call | solution.py:200
  123.8 10.9 %section_ahead.3.refs_0_ = bf16[256,512]{1,0:T(8,128)(2,1)} custom-call(s32[1]{0:T(128)} %bitcast.refs_0_, s32[4]{0:T(128)} %reshape.252.refs_1_, bf16[2048,512]{1,0:T(8,128)(2,1)} %bitcast.21.refs_2_, s32[2048,1]{1,0:T(8,128)} %copy.61.refs_3_, s32[1,512]{1,0:T(1,128)} %get-tuple-element.103.refs_4_, bf16[256,512]{1,0:T(8,128)(2,1)} %get-tuple-element.47.refs_5_, ...), custom_call_target="tpu_custom_call" | custom-call | flops 8589934592 | bytes 4194304 | tf_op jit(solution)/shard_map/section_ahead/pallas_call | solution.py:200
  134.7 25.9 %exchange_ahead_back.1 = (bf16[256,512]{1,0:T(8,128)(2,1)}, f32[1,512]{1,0:T(1,128)}, bf16[256,512]{1,0:T(8,128)(2,1)}) custom-call(bf16[256,512]{1,0:T(8,128)(2,1)} %section_ahead.3.refs_0_, f32[256,512]{1,0:T(8,128)} %get-tuple-element.48.refs_1_, f32[1,512]{1,0:T(1,128)} %get-tuple-element.49.refs_2_, bf16[256,512]{1,0:T(8,128)(2,1)} %get-tuple-element.42.refs_5_.refs_3_, ...), custom_call_target="tpu_custom_call" | custom-call | tf_op jit(solution)/shard_map/exchange_ahead_back/pallas_call | solution.py:401
  160.6 3.9 %section_back.5 = (bf16[256,512]{1,0:T(8,128)(2,1)}, bf16[2048,512]{1,0:T(8,128)(2,1)}, f32[256,512]{1,0:T(8,128)}, f32[1,512]{1,0:T(1,128)}, f32[256,1]{1,0:T(8,128)}, /*index=5*/f32[256,1]{1,0:T(8,128)}) custom-call(s32[1]{0:T(128)} %bitcast.refs_0_, s32[4]{0:T(128)} %reshape.252.refs_1_, bf16[2048,512]{1,0:T(8,128)(2,1)} %bitcast.21.refs_2_, ...), custom_call_target="tpu_custom_call" | custom-call | flops 19327352832 | bytes 4194304 | tf_op jit(solution)/shard_map/section_back/pallas_call | solution.py:200
  164.6 18.8 %section_back.6 = (bf16[256,512]{1,0:T(8,128)(2,1)}, bf16[2048,512]{1,0:T(8,128)(2,1)}, f32[256,512]{1,0:T(8,128)}, f32[1,512]{1,0:T(1,128)}, f32[256,1]{1,0:T(8,128)}, /*index=5*/f32[256,1]{1,0:T(8,128)}) custom-call(s32[1]{0:T(128)} %bitcast.refs_0_, s32[4]{0:T(128)} %reshape.248.refs_1_, bf16[2048,512]{1,0:T(8,128)(2,1)} %bitcast.75, ...), custom_call_target="tpu_custom_call" | custom-call | flops 19327352832 | bytes 4194304 | tf_op jit(solution)/shard_map/section_back/pallas_call | solution.py:200
  183.4 14.9 %exchange_back.1.refs_9_ = bf16[256,512]{1,0:T(8,128)(2,1)} custom-call(f32[256,512]{1,0:T(8,128)} %get-tuple-element.58.refs_0_, f32[1,512]{1,0:T(1,128)} %get-tuple-element.59.refs_1_, bf16[256,512]{1,0:T(8,128)(2,1)} %get-tuple-element.50.refs_5_.refs_2_, f32[1,512]{1,0:T(1,128)} %get-tuple-element.51.refs_6_.refs_3_), custom_call_target="tpu_custom_call" | custom-call | tf_op jit(solution)/shard_map/exchange_back/pallas_call | solution.py:401
  198.3 3.1 broadcast_select_fusion.1
  201.4 6.4 %all-to-all-start.2 = ((bf16[16,128,512]{2,1,0:T(8,128)(2,1)}), bf16[16,128,512]{2,1,0:T(8,128)(2,1)S(1)}, u32[]{:S(2)}, u32[]{:S(2)}) async-start(bf16[16,128,512]{2,1,0:T(8,128)(2,1)} %bitcast.28), calls=%async_computation.2 | async-start | bytes 4194304 | tf_op jit(solution)/shard_map/all_to_all | solution.py:528
  207.9 18.8 %section_back.7 = (bf16[256,512]{1,0:T(8,128)(2,1)}, bf16[2048,512]{1,0:T(8,128)(2,1)}, f32[256,512]{1,0:T(8,128)}, f32[1,512]{1,0:T(1,128)}, f32[256,1]{1,0:T(8,128)}, /*index=5*/f32[256,1]{1,0:T(8,128)}) custom-call(s32[1]{0:T(128)} %bitcast.refs_0_, s32[4]{0:T(128)} %reshape.252.refs_1_, bf16[2048,512]{1,0:T(8,128)(2,1)} %bitcast.21.refs_2_, ...), custom_call_target="tpu_custom_call" | custom-call | flops 19327352832 | bytes 4194304 | tf_op jit(solution)/shard_map/section_back/pallas_call | solution.py:200
  226.7 3.1 broadcast_select_fusion
  229.8 25.5 %all-to-all-done.2.refs_0_ = bf16[16,128,512]{2,1,0:T(8,128)(2,1)S(1)} async-done(((bf16[16,128,512]{2,1,0:T(8,128)(2,1)}), bf16[16,128,512]{2,1,0:T(8,128)(2,1)S(1)}, u32[]{:S(2)}, u32[]{:S(2)}) %all-to-all-start.2) | async-done | bytes 2097184 | tf_op jit(solution)/shard_map/all_to_all | solution.py:528
  256.6 4.9 %all-to-all-start.3 = ((bf16[16,128,512]{2,1,0:T(8,128)(2,1)}), bf16[16,128,512]{2,1,0:T(8,128)(2,1)}, u32[]{:S(2)}, u32[]{:S(2)}) async-start(bf16[16,128,512]{2,1,0:T(8,128)(2,1)} %bitcast.29), calls=%async_computation.3 | async-start | bytes 4194304 | tf_op jit(solution)/shard_map/all_to_all | solution.py:528
  264.1 44.9 %all-to-all-done.3.refs_1_ = bf16[16,128,512]{2,1,0:T(8,128)(2,1)} async-done(((bf16[16,128,512]{2,1,0:T(8,128)(2,1)}), bf16[16,128,512]{2,1,0:T(8,128)(2,1)}, u32[]{:S(2)}, u32[]{:S(2)}) %all-to-all-start.3) | async-done | bytes 2097184 | tf_op jit(solution)/shard_map/all_to_all | solution.py:528
  309.0 4.7 %gather.1 = bf16[1,2,128,8192]{3,2,1,0:T(8,128)(2,1)} custom-call(bf16[16,128,512]{2,1,0:T(8,128)(2,1)} %copy-done, bf16[16,128,512]{2,1,0:T(8,128)(2,1)} %all-to-all-done.3.refs_1_), custom_call_target="tpu_custom_call" | custom-call | tf_op jit(solution)/shard_map/gather/pallas_call | solution.py:444
  (79 shorter events, 13.0 us)
Async XLA Ops:
  14.3 53.9 %all-to-all-start = ((bf16[16,128,512]{2,1,0:T(8,128)(2,1)}), bf16[16,128,512]{2,1,0:T(8,128)(2,1)S(1)}, u32[]{:S(2)}, u32[]{:S(2)}) async-start(bf16[16,128,512]{2,1,0:T(8,128)(2,1)} %scatter.3), calls=%async_computation | async-start | bytes 4194304 | tf_op jit(solution)/shard_map/all_to_all | solution.py:484
  20.7 3.1 copy-start.19
  20.7 4.0 %copy-start.17 = (s32[2,2048]{1,0:T(2,128)S(1)}, s32[2,2048]{1,0:T(2,128)}, u32[]{:S(2)}) copy-start(s32[2,2048]{1,0:T(2,128)} %param.10) | copy-start | bytes 49156
  25.0 50.0 %copy-start.20 = (f32[1,256]{1,0:T(1,128)S(1)}, f32[1,256]{1,0:T(1,128)}, u32[]{:S(2)}) copy-start(f32[1,256]{1,0:T(1,128)} %param.11) | copy-start | bytes 3076
  25.0 50.8 %copy-start.21 = (f32[1,256]{1,0:T(1,128)S(1)}, f32[1,256]{1,0:T(1,128)}, u32[]{:S(2)}) copy-start(f32[1,256]{1,0:T(1,128)} %param.12) | copy-start | bytes 3076
  25.0 51.6 %copy-start.6 = (bf16[2,512,256]{2,1,0:T(8,128)(2,1)S(1)}, bf16[2,512,256]{2,1,0:T(8,128)(2,1)}, u32[]{:S(2)}) copy-start(bf16[2,512,256]{2,1,0:T(8,128)(2,1)} %param.13) | copy-start | bytes 1572868
  68.2 4.9 %copy-start.3 = (bf16[16,128,512]{2,1,0:T(8,128)(2,1)}, bf16[16,128,512]{2,1,0:T(8,128)(2,1)S(1)}, u32[]{:S(2)}) copy-start(bf16[16,128,512]{2,1,0:T(8,128)(2,1)S(1)} %all-to-all-done) | copy-start | bytes 6291460
  68.2 55.6 %all-to-all-start.1 = ((bf16[16,128,512]{2,1,0:T(8,128)(2,1)}), bf16[16,128,512]{2,1,0:T(8,128)(2,1)}, u32[]{:S(2)}, u32[]{:S(2)}) async-start(bf16[16,128,512]{2,1,0:T(8,128)(2,1)} %scatter.2), calls=%async_computation.1 | async-start | bytes 4194304 | tf_op jit(solution)/shard_map/all_to_all | solution.py:484
  73.1 6.6 %copy-start.18 = (f32[2,512]{1,0:T(2,128)S(1)}, f32[2,512]{1,0:T(2,128)}, u32[]{:S(2)}) copy-start(f32[2,512]{1,0:T(2,128)} %row_totals.1) | copy-start | bytes 12292
  164.6 33.7 %copy-start.2 = (bf16[2048,512]{1,0:T(8,128)(2,1)S(1)}, bf16[2048,512]{1,0:T(8,128)(2,1)}, u32[]{:S(2)}) copy-start(bf16[2048,512]{1,0:T(8,128)(2,1)} %get-tuple-element.57) | copy-start | bytes 6291460
  201.4 53.9 %all-to-all-start.2 = ((bf16[16,128,512]{2,1,0:T(8,128)(2,1)}), bf16[16,128,512]{2,1,0:T(8,128)(2,1)S(1)}, u32[]{:S(2)}, u32[]{:S(2)}) async-start(bf16[16,128,512]{2,1,0:T(8,128)(2,1)} %bitcast.28), calls=%async_computation.2 | async-start | bytes 4194304 | tf_op jit(solution)/shard_map/all_to_all | solution.py:528
  207.9 18.8 %copy-start.1 = (bf16[2048,512]{1,0:T(8,128)(2,1)S(1)}, bf16[2048,512]{1,0:T(8,128)(2,1)}, u32[]{:S(2)}) copy-start(bf16[2048,512]{1,0:T(8,128)(2,1)} %get-tuple-element.62) | copy-start | bytes 6291460
  255.3 1.3 copy-start
  255.3 6.3 %copy-start.4 = (bf16[256,512]{1,0:T(8,128)(2,1)S(1)}, bf16[256,512]{1,0:T(8,128)(2,1)}, u32[]{:S(2)}) copy-start(bf16[256,512]{1,0:T(8,128)(2,1)} %section_ahead.2.refs_0_) | copy-start | bytes 786436
  255.3 6.3 %copy-start.7 = (bf16[256,512]{1,0:T(8,128)(2,1)S(1)}, bf16[256,512]{1,0:T(8,128)(2,1)}, u32[]{:S(2)}) copy-start(bf16[256,512]{1,0:T(8,128)(2,1)} %get-tuple-element.44) | copy-start | bytes 786436
  255.3 6.3 %copy-start.5 = (bf16[256,512]{1,0:T(8,128)(2,1)S(1)}, bf16[256,512]{1,0:T(8,128)(2,1)}, u32[]{:S(2)}) copy-start(bf16[256,512]{1,0:T(8,128)(2,1)} %section_ahead.3.refs_0_) | copy-start | bytes 786436
  255.3 6.4 %copy-start.8 = (bf16[256,512]{1,0:T(8,128)(2,1)S(1)}, bf16[256,512]{1,0:T(8,128)(2,1)}, u32[]{:S(2)}) copy-start(bf16[256,512]{1,0:T(8,128)(2,1)} %get-tuple-element.52) | copy-start | bytes 786436
  256.6 52.4 %all-to-all-start.3 = ((bf16[16,128,512]{2,1,0:T(8,128)(2,1)}), bf16[16,128,512]{2,1,0:T(8,128)(2,1)}, u32[]{:S(2)}, u32[]{:S(2)}) async-start(bf16[16,128,512]{2,1,0:T(8,128)(2,1)} %bitcast.29), calls=%async_computation.3 | async-start | bytes 4194304 | tf_op jit(solution)/shard_map/all_to_all | solution.py:528
  261.5 1.3 copy-start.10
  261.5 1.3 copy-start.12
  261.5 1.9 copy-start.9
  261.6 1.9 copy-start.11
  261.6 1.9 copy-start.13
  261.6 1.9 copy-start.15
  (2 other events, 2.5 us)

commit v4 on v3

--- a/solution.py
+++ b/solution.py
@@ -26,13 +26,13 @@
     return lax.dot_general(a, b, (((1,), (1,)), ((), ())), preferred_element_type=jnp.float32)
 
 
-def attention_kernel(backward, active, width, *refs):
+def attention_kernel(backward, width, *refs):
     if backward:
-        (phase_ref, bound_ref, kv_ref, kseg_ref, qseg_ref, x_ref, total_ref, qg_ref, og_ref, g_ref,
+        (bound_ref, kv_ref, kseg_ref, qseg_ref, x_ref, total_ref, qg_ref, og_ref, g_ref,
          y_ref, gkv_ref, part_ref, cross_ref, gqg_ref, gog_ref,
          score_ref, top_ref, kvt_ref, pair_ref, gprob_ref, acc_ref) = refs
     else:
-        (phase_ref, bound_ref, kv_ref, kseg_ref, qseg_ref, x_ref, total_ref, qg_ref, og_ref,
+        (bound_ref, kv_ref, kseg_ref, qseg_ref, x_ref, total_ref, qg_ref, og_ref,
          y_ref, score_ref, top_ref, kvt_ref, pair_ref) = refs
     enc = kv_ref.shape[0]
     feats, rows = x_ref.shape
@@ -166,10 +166,10 @@
 
             lax.fori_loop(0, enc // chunk, store, 0)
 
-    pl.when(phase_ref[0] == active)(work)
-
-
-def attention(backward, active, width, phase, bounds, kv, kseg, qseg, x, total, qg, og, g=None):
+    work()
+
+
+def attention(backward, width, bounds, kv, kseg, qseg, x, total, qg, og, g=None):
     enc = kv.shape[0]
     feats, rows = x.shape
     block = min(QROWS, rows)
@@ -181,7 +181,7 @@
         pltpu.VMEM((heads, 2 * HEAD, enc), jnp.bfloat16),
         pltpu.VMEM((heads, 2 * HEAD, 2 * block if backward else block), jnp.bfloat16),
     ]
-    operands = [phase, bounds, kv, kseg, qseg, x, total, qg, og]
+    operands = [bounds, kv, kseg, qseg, x, total, qg, og]
     if backward:
         operands.append(g)
         shapes += [
@@ -198,9 +198,9 @@
     smem = pl.BlockSpec(memory_space=pltpu.SMEM)
     vmem = pl.BlockSpec(memory_space=pltpu.VMEM)
     return pl.pallas_call(
-        functools.partial(attention_kernel, backward, active, width),
+        functools.partial(attention_kernel, backward, width),
         out_shape=shapes,
-        in_specs=[smem, smem] + [vmem] * (len(operands) - 2),
+        in_specs=[smem] + [vmem] * (len(operands) - 1),
         out_specs=[vmem] * len(shapes),
         scratch_shapes=scratch,
         compiler_params=pltpu.CompilerParams(vmem_limit_bytes=VMEM_BYTES),
@@ -467,7 +467,6 @@
     own_enc = enc_kv.shape[2]
     enc = enc_seg.shape[1]
     width = feats * n
-    flag = phase.astype(jnp.int32).reshape(1)
     qg = q_gain.reshape(feats, 1)
     og = o_gain.reshape(feats, 1)
     inputs = dec_in.transpose(0, 2, 1)
@@ -486,7 +485,7 @@
     calls, x0s, t0s = [], [], []
     for m in range(micro):
         calls.append(functools.partial(
-            attention, width=width, phase=flag, bounds=doc_bounds(dec_seg[m], enc_seg[m]),
+            attention, width=width, bounds=doc_bounds(dec_seg[m], enc_seg[m]),
             kv=scattered[m].reshape(enc, 2 * feats), kseg=enc_seg[m].reshape(enc, 1),
             qseg=dec_seg[m].reshape(1, rows), qg=qg, og=og,
         ))
@@ -494,28 +493,50 @@
         t0s.append(first_totals[m].reshape(1, rows))
     outs, grads, gqgs, gogs = [], [], [], []
 
+    def section_ahead(m, x0):
+        def run():
+            return calls[m](False, x=x0, total=t0s[m])[0]
+
+        return lax.cond(phase == 0, run, lambda: x0)
+
+    def section_back(m, x1, total1):
+        def run():
+            return tuple(calls[m](True, x=x1, total=total1, g=wanted[m]))
+
+        def rest():
+            column = jnp.zeros((feats, 1), jnp.float32)
+            return (x1, calls[m].keywords["kv"], jnp.zeros((feats, rows), jnp.float32), total1, column, column)
+
+        return lax.cond(phase == 1, run, rest)
+
     def finish(m, y0, first, g0):
+        def run():
+            _, gkv0, _, _, gqg0, gog0 = calls[m](True, x=x0s[m], total=t0s[m], g=g0)
+            return (gkv0, gqg0, gog0)
+
         y1, gkv1, gqg1, gog1 = first
-        _, gkv0, _, _, gqg0, gog0 = calls[m](True, 0, x=x0s[m], total=t0s[m], g=g0)
         outs.append(jnp.where(phase == 0, y0, y1).T)
-        grads.append(jnp.where(phase == 0, gkv0, gkv1).reshape(n, own_enc, 2 * feats))
-        gqgs.append(jnp.where(phase == 0, gqg0, gqg1))
-        gogs.append(jnp.where(phase == 0, gog0, gog1))
-
-    y0 = calls[0](False, 0, x=x0s[0], total=t0s[0])[0]
+        gkv, gqg, gog = lax.cond(phase == 0, run, lambda: (gkv1, gqg1, gog1))
+        grads.append(gkv.reshape(n, own_enc, 2 * feats))
+        gqgs.append(gqg)
+        gogs.append(gog)
+
+    y0 = section_ahead(0, x0s[0])
     x1, total1 = exchange(n, width, y=y0)
     waiting = None
     for m in range(micro):
-        y1, gkv1, part, cross, gqg1, gog1 = calls[m](True, 1, x=x1, total=total1, g=wanted[m])
+        y1, gkv1, part, cross, gqg1, gog1 = section_back(m, x1, total1)
         if waiting is not None:
             waiting[2], part = lax.optimization_barrier((waiting[2], part))
             finish(m - 1, *waiting)
         waiting = [y0, (y1, gkv1, gqg1, gog1), None]
         if m + 1 < micro:
             x_next, part = lax.optimization_barrier((x0s[m + 1], part))
-            y0 = calls[m + 1](False, 0, x=x_next, total=t0s[m + 1])[0]
+            y0 = section_ahead(m + 1, x_next)
             x1, total1, waiting[2] = exchange(n, width, y=y0, back=(part, cross, x1, total1))
         else:
+            if grads:
+                cross, grads[-1] = lax.optimization_barrier((cross, grads[-1]))
             waiting[2] = exchange(n, width, back=(part, cross, x1, total1))[0]
             if grads:
                 grads[-1], waiting[2] = lax.optimization_barrier((grads[-1], waiting[2]))

time: 315 us -> 322 us (1.022)
  local copies, waits for them, and re-layouts: 13.1 us -> 36.4 us
  Pallas kernels: 155 us -> 140 us
  other arithmetic: 8.94 us -> 2.84 us
    another operation x0 -> x18, local copies, waits for them, and re-layouts: none -> 17.5 us
    pallas_call x6 -> x4, Pallas kernels: 67.2 us -> 56.2 us  [attention(): pl.pallas_call(functools.partial(attention_kernel, backward, width), out_...]
    cond x0 -> x10, local copies, waits for them, and re-layouts: none -> 10 us
    select_n x2, other arithmetic: 6.25 us -> 0.02 us  [doc_bounds(): below // chunk]
  transfers between devices with their start and end apart: 4 -> 4, of which waited for: 3 -> 3; matrix products, arithmetic and copies ran while one was open for 5% -> 6% of each run, Pallas kernels for 20% -> 19%
where the time goes in v4:
time: 322 us; the launch traced here: 320 us
  Pallas kernels  140 us (43%)
  waiting for transfers between devices  116 us (36%)
  local copies, waits for them, and re-layouts  36.4 us (11%)
  starting transfers between devices  23 us (7%)
    all_to_all x2, waiting for transfers between devices, local(): lax.all_to_all(grad, 'seq', split_axis=0, concat_axis=0, tiled=True)  71.6 us
    pallas_call x3, Pallas kernels, exchange(): pl.pallas_call(functools.partial(exchange_kernel, n, width, ahead, back i...  64.9 us
    pallas_call x4, Pallas kernels, attention(): pl.pallas_call(functools.partial(attention_kernel, backward, width), out_...  56.2 us
    all_to_all x2, waiting for transfers between devices, local(): lax.all_to_all(blocks, 'seq', split_axis=0, concat_axis=0, tiled=True)  44.4 us
    another operation x18, local copies, waits for them, and re-layouts  17.5 us
    all_to_all x2, starting transfers between devices, local(): lax.all_to_all(grad, 'seq', split_axis=0, concat_axis=0, tiled=True)  11.6 us
    all_to_all x2, starting transfers between devices, local(): lax.all_to_all(blocks, 'seq', split_axis=0, concat_axis=0, tiled=True)  11.4 us
    cond x6, local copies, waits for them, and re-layouts  9.51 us
  transfers between devices with their start and end apart: 4, of which 3 were waited for; matrix products, arithmetic and copies ran while one was open for 6% of the time, Pallas kernels for 19%

profile of v4, /device:TPU:13, one launch (start us, length us, event | category | flops | bytes accessed | tf_op | source)
XLA Modules:
  0.0 320.0 jit_solution(4573817859810388695)
XLA Ops:
  2.6 8.6 %row_totals.1 = f32[2,512]{1,0:T(2,128)} custom-call(f32[2,512]{1,0:T(2,128)} %multiply_reduce_fusion.part_ref), custom_call_target="tpu_custom_call" | custom-call | tf_op jit(solution)/shard_map/row_totals/pallas_call | solution.py:254
  11.2 3.1 scatter.3
  14.3 6.5 %all-to-all-start = ((bf16[16,128,512]{2,1,0:T(8,128)(2,1)}), bf16[16,128,512]{2,1,0:T(8,128)(2,1)S(1)}, u32[]{:S(2)}, u32[]{:S(2)}) async-start(bf16[16,128,512]{2,1,0:T(8,128)(2,1)} %scatter.3), calls=%async_computation | async-start | bytes 4194304 | tf_op jit(solution)/shard_map/all_to_all | solution.py:483
  23.8 44.4 %all-to-all-done = bf16[16,128,512]{2,1,0:T(8,128)(2,1)S(1)} async-done(((bf16[16,128,512]{2,1,0:T(8,128)(2,1)}), bf16[16,128,512]{2,1,0:T(8,128)(2,1)S(1)}, u32[]{:S(2)}, u32[]{:S(2)}) %all-to-all-start) | async-done | bytes 2097184 | tf_op jit(solution)/shard_map/all_to_all | solution.py:483
  69.5 4.9 %all-to-all-start.1 = ((bf16[16,128,512]{2,1,0:T(8,128)(2,1)}), bf16[16,128,512]{2,1,0:T(8,128)(2,1)S(1)}, u32[]{:S(2)}, u32[]{:S(2)}) async-start(bf16[16,128,512]{2,1,0:T(8,128)(2,1)} %scatter.2), calls=%async_computation.1 | async-start | bytes 4194304 | tf_op jit(solution)/shard_map/all_to_all | solution.py:483
  79.8 13.2 %conditional.6 = (bf16[256,512]{1,0:T(8,128)(2,1)S(1)}) conditional(s32[]{:T(128)} %convert_element_type.25, bf16[256,512]{1,0:T(8,128)(2,1)} %get-tuple-element.416, (s32[4]{0:T(128)S(1)}, bf16[2048,512]{1,0:T(8,128)(2,1)}, s32[2048,1]{0,1:T(1,128)S(1)}, s32[1,512]{1,0:T(1,128)S(1)}, bf16[256,512]{1,0:T(8,128)(2,1)}, /*index=5*/f32[1,512]{1,0:T(1,128)}, ...), branch_computations={%region_3.4_spmd, %region_4.5_spmd} | conditional | flops 8589934592 | bytes 4214792 | solution.py:500
  82.8 10.2 %section_ahead.2 = bf16[256,512]{1,0:T(8,128)(2,1)S(1)} custom-call(s32[4]{0:T(128)S(1)} %get-tuple-element.150.refs_0_, bf16[2048,512]{1,0:T(8,128)(2,1)} %get-tuple-element.151.refs_1_, s32[2048,1]{1,0:T(8,128)} %copy.57.refs_2_, s32[1,512]{1,0:T(1,128)S(1)} %get-tuple-element.153.refs_3_, bf16[256,512]{1,0:T(8,128)(2,1)} %get-tuple-element.154.refs_4_, ...), custom_call_target="tpu_custom_call" | custom-call | flops 8589934592 | bytes 4194304 | tf_op jit(solution)/shard_map/cond/branch_1_fun/section_ahead/pallas_call | solution.py:200
  93.0 28.4 %exchange_ahead.1 = (bf16[256,512]{1,0:T(8,128)(2,1)}, f32[1,512]{1,0:T(1,128)}) custom-call(bf16[256,512]{1,0:T(8,128)(2,1)S(1)} %get-tuple-element.470.refs_0_), custom_call_target="tpu_custom_call" | custom-call | tf_op jit(solution)/shard_map/exchange_ahead/pallas_call | solution.py:401
  121.5 6.8 %conditional.7 = ((bf16[256,512]{1,0:T(8,128)(2,1)S(1)}, bf16[2048,512]{1,0:T(8,128)(2,1)}, f32[256,512]{1,0:T(8,128)}, f32[1,512]{1,0:T(1,128)}, f32[256,1]{1,0:T(8,128)}, /*index=5*/f32[256,1]{1,0:T(8,128)S(1)})) conditional(s32[]{:T(128)} %convert_element_type.29, (bf16[256,512]{1,0:T(8,128)(2,1)}, bf16[2048,512]{1,0:T(8,128)(2,1)}, ...), branch_computations={%region_5.6_spmd, %region_6.7_spmd} | conditional | flops 19327352832 | bytes 5249092 | solution.py:510
  123.7 3.0 copy.90
  128.3 13.8 %conditional.8 = (bf16[256,512]{1,0:T(8,128)(2,1)S(1)}) conditional(s32[]{:T(128)} %convert_element_type.25, bf16[256,512]{1,0:T(8,128)(2,1)} %get-tuple-element.262, (s32[4]{0:T(128)}, bf16[2048,512]{1,0:T(8,128)(2,1)S(1)}, s32[2048,1]{0,1:T(1,128)S(1)}, s32[1,512]{1,0:T(1,128)}, bf16[256,512]{1,0:T(8,128)(2,1)}, /*index=5*/f32[1,512]{1,0:T(1,128)}, ...), branch_computations={%region_9.10_spmd, %region_10.11_spmd} | conditional | flops 8589934592 | bytes 4214792 | solution.py:500
  132.6 9.5 %section_ahead.3 = bf16[256,512]{1,0:T(8,128)(2,1)S(1)} custom-call(s32[4]{0:T(128)} %get-tuple-element.170.refs_0_, bf16[2048,512]{1,0:T(8,128)(2,1)S(1)} %get-tuple-element.171.refs_1_, s32[2048,1]{1,0:T(8,128)} %copy.69.refs_2_, s32[1,512]{1,0:T(1,128)} %get-tuple-element.173.refs_3_, bf16[256,512]{1,0:T(8,128)(2,1)} %get-tuple-element.174.refs_4_, ...), custom_call_target="tpu_custom_call" | custom-call | flops 8589934592 | bytes 4194304 | tf_op jit(solution)/shard_map/cond/branch_1_fun/section_ahead/pallas_call | solution.py:200
  142.1 21.6 %exchange_ahead_back.1 = (bf16[256,512]{1,0:T(8,128)(2,1)}, f32[1,512]{1,0:T(1,128)}, bf16[256,512]{1,0:T(8,128)(2,1)}) custom-call(bf16[256,512]{1,0:T(8,128)(2,1)S(1)} %get-tuple-element.472.refs_0_, f32[256,512]{1,0:T(8,128)} %get-tuple-element.264.refs_1_, f32[1,512]{1,0:T(1,128)} %get-tuple-element.265.refs_2_, ...), custom_call_target="tpu_custom_call" | custom-call | tf_op jit(solution)/shard_map/exchange_ahead_back/pallas_call | solution.py:401
  163.8 5.9 %conditional.9 = ((bf16[256,512]{1,0:T(8,128)(2,1)}, bf16[2048,512]{1,0:T(8,128)(2,1)}, f32[256,512]{1,0:T(8,128)S(1)}, f32[1,512]{1,0:T(1,128)}, f32[256,1]{1,0:T(8,128)}, /*index=5*/f32[256,1]{1,0:T(8,128)})) conditional(s32[]{:T(128)} %convert_element_type.29, (bf16[256,512]{1,0:T(8,128)(2,1)}, bf16[2048,512]{1,0:T(8,128)(2,1)S(1)}, ...), branch_computations={%region_11.12_spmd, %region_12.13_spmd} | conditional | flops 19327352832 | bytes 5249092 | solution.py:510
  169.6 22.9 %conditional.10 = ((f32[256,1]{1,0:T(8,128)}, f32[256,1]{1,0:T(8,128)S(1)}, bf16[2048,512]{1,0:T(8,128)(2,1)})) conditional(s32[]{:T(128)} %convert_element_type.25, (f32[256,1]{1,0:T(8,128)}, f32[256,1]{1,0:T(8,128)S(1)}, bf16[2048,512]{1,0:T(8,128)(2,1)}) %tuple.75, (s32[4]{0:T(128)}, bf16[2048,512]{1,0:T(8,128)(2,1)}, s32[2048,1]{0,1:T(1,128)S(1)}, ...), branch_computations={%region_13.14_spmd, %region_14.15_spmd} | conditional | flops 19327352832 | bytes 4214816 | solution.py:519
  174.0 18.6 %section_back.6 = (bf16[256,512]{1,0:T(8,128)(2,1)}, bf16[2048,512]{1,0:T(8,128)(2,1)}, f32[256,512]{1,0:T(8,128)}, f32[1,512]{1,0:T(1,128)}, f32[256,1]{1,0:T(8,128)}, /*index=5*/f32[256,1]{1,0:T(8,128)S(1)}) custom-call(s32[4]{0:T(128)} %get-tuple-element.190.refs_0_, bf16[2048,512]{1,0:T(8,128)(2,1)} %get-tuple-element.191.refs_1_, ...), custom_call_target="tpu_custom_call" | custom-call | flops 19327352832 | bytes 4194304 | tf_op jit(solution)/shard_map/cond/branch_1_fun/section_back/pallas_call | solution.py:200
  192.5 14.8 %exchange_back.1 = bf16[256,512]{1,0:T(8,128)(2,1)} custom-call(f32[256,512]{1,0:T(8,128)S(1)} %get-tuple-element.281.refs_0_, f32[1,512]{1,0:T(1,128)} %get-tuple-element.282.refs_1_, bf16[256,512]{1,0:T(8,128)(2,1)} %get-tuple-element.266.refs_2_, f32[1,512]{1,0:T(1,128)} %get-tuple-element.267.refs_3_), custom_call_target="tpu_custom_call" | custom-call | tf_op jit(solution)/shard_map/exchange_back/pallas_call | solution.py:401
  207.4 6.6 %all-to-all-start.2 = ((bf16[16,128,512]{2,1,0:T(8,128)(2,1)}), bf16[16,128,512]{2,1,0:T(8,128)(2,1)}, u32[]{:S(2)}, u32[]{:S(2)}) async-start(bf16[16,128,512]{2,1,0:T(8,128)(2,1)} %bitcast.79), calls=%async_computation.2 | async-start | bytes 4194304 | tf_op jit(solution)/shard_map/all_to_all | solution.py:549
  214.0 20.9 %conditional.11 = ((f32[256,1]{1,0:T(8,128)}, f32[256,1]{1,0:T(8,128)}, bf16[2048,512]{1,0:T(8,128)(2,1)})) conditional(s32[]{:T(128)} %convert_element_type.25, (f32[256,1]{1,0:T(8,128)}, f32[256,1]{1,0:T(8,128)}, bf16[2048,512]{1,0:T(8,128)(2,1)}) %tuple.74, (s32[4]{0:T(128)}, bf16[2048,512]{1,0:T(8,128)(2,1)S(1)}, s32[2048,1]{0,1:T(1,128)S(1)}, ...), branch_computations={%region_15.16_spmd, %region_16.17_spmd} | conditional | flops 19327352832 | bytes 4214816 | solution.py:519
  217.0 17.9 %section_back.7 = (bf16[256,512]{1,0:T(8,128)(2,1)}, bf16[2048,512]{1,0:T(8,128)(2,1)}, f32[256,512]{1,0:T(8,128)}, f32[1,512]{1,0:T(1,128)}, f32[256,1]{1,0:T(8,128)}, /*index=5*/f32[256,1]{1,0:T(8,128)}) custom-call(s32[4]{0:T(128)} %get-tuple-element.202.refs_0_, bf16[2048,512]{1,0:T(8,128)(2,1)S(1)} %get-tuple-element.203.refs_1_, ...), custom_call_target="tpu_custom_call" | custom-call | flops 19327352832 | bytes 4194304 | tf_op jit(solution)/shard_map/cond/branch_1_fun/section_back/pallas_call | solution.py:200
  234.9 26.6 %all-to-all-done.2.refs_0_ = bf16[16,128,512]{2,1,0:T(8,128)(2,1)} async-done(((bf16[16,128,512]{2,1,0:T(8,128)(2,1)}), bf16[16,128,512]{2,1,0:T(8,128)(2,1)}, u32[]{:S(2)}, u32[]{:S(2)}) %all-to-all-start.2) | async-done | bytes 2097184 | tf_op jit(solution)/shard_map/all_to_all | solution.py:549
  261.5 5.0 %all-to-all-start.3 = ((bf16[16,128,512]{2,1,0:T(8,128)(2,1)}), bf16[16,128,512]{2,1,0:T(8,128)(2,1)S(1)}, u32[]{:S(2)}, u32[]{:S(2)}) async-start(bf16[16,128,512]{2,1,0:T(8,128)(2,1)} %bitcast.80), calls=%async_computation.3 | async-start | bytes 4194304 | tf_op jit(solution)/shard_map/all_to_all | solution.py:549
  268.9 45.0 %all-to-all-done.3.refs_1_ = bf16[16,128,512]{2,1,0:T(8,128)(2,1)S(1)} async-done(((bf16[16,128,512]{2,1,0:T(8,128)(2,1)}), bf16[16,128,512]{2,1,0:T(8,128)(2,1)S(1)}, u32[]{:S(2)}, u32[]{:S(2)}) %all-to-all-start.3) | async-done | bytes 2097184 | tf_op jit(solution)/shard_map/all_to_all | solution.py:549
  315.3 4.7 %gather.1 = bf16[1,2,128,8192]{3,2,1,0:T(8,128)(2,1)} custom-call(bf16[16,128,512]{2,1,0:T(8,128)(2,1)} %all-to-all-done.2.refs_0_, bf16[16,128,512]{2,1,0:T(8,128)(2,1)} %copy-done.1), custom_call_target="tpu_custom_call" | custom-call | tf_op jit(solution)/shard_map/gather/pallas_call | solution.py:444
  (93 shorter events, 39.2 us)
Async XLA Ops:
  14.3 53.9 %all-to-all-start = ((bf16[16,128,512]{2,1,0:T(8,128)(2,1)}), bf16[16,128,512]{2,1,0:T(8,128)(2,1)S(1)}, u32[]{:S(2)}, u32[]{:S(2)}) async-start(bf16[16,128,512]{2,1,0:T(8,128)(2,1)} %scatter.3), calls=%async_computation | async-start | bytes 4194304 | tf_op jit(solution)/shard_map/all_to_all | solution.py:483
  23.8 50.7 %copy-start.14 = (s32[2,512]{1,0:T(2,128)S(1)}, s32[2,512]{1,0:T(2,128)}, u32[]{:S(2)}) copy-start(s32[2,512]{1,0:T(2,128)} %param.21) | copy-start | bytes 12292
  23.8 51.8 %copy-start.12 = (s32[2,2048]{1,0:T(2,128)S(1)}, s32[2,2048]{1,0:T(2,128)}, u32[]{:S(2)}) copy-start(s32[2,2048]{1,0:T(2,128)} %param.22) | copy-start | bytes 49156
  23.8 54.5 %copy-start.13 = (f32[2,512]{1,0:T(2,128)S(1)}, f32[2,512]{1,0:T(2,128)}, u32[]{:S(2)}) copy-start(f32[2,512]{1,0:T(2,128)} %row_totals.1) | copy-start | bytes 12292
  68.2 1.4 copy-start
  69.5 58.7 %all-to-all-start.1 = ((bf16[16,128,512]{2,1,0:T(8,128)(2,1)}), bf16[16,128,512]{2,1,0:T(8,128)(2,1)S(1)}, u32[]{:S(2)}, u32[]{:S(2)}) async-start(bf16[16,128,512]{2,1,0:T(8,128)(2,1)} %scatter.2), calls=%async_computation.1 | async-start | bytes 4194304 | tf_op jit(solution)/shard_map/all_to_all | solution.py:483
  74.5 5.4 %copy-start.8 = (f32[1,256]{1,0:T(1,128)S(1)}, f32[1,256]{1,0:T(1,128)}, u32[]{:S(2)}) copy-start(f32[1,256]{1,0:T(1,128)} %param.23) | copy-start | bytes 3076
  74.5 5.3 %copy-start.10 = (f32[1,256]{1,0:T(1,128)S(1)}, f32[1,256]{1,0:T(1,128)}, u32[]{:S(2)}) copy-start(f32[1,256]{1,0:T(1,128)} %param.24) | copy-start | bytes 3076
  75.1 46.3 %copy-start.15 = (s32[1,512]{1,0:T(1,128)}, s32[1,512]{1,0:T(1,128)S(1)}, u32[]{:S(2)}) copy-start(s32[1,512]{1,0:T(1,128)S(1)} %get-tuple-element.425) | copy-start | bytes 6148
  76.1 45.3 %copy-start.17 = (s32[4]{0:T(128)}, s32[4]{0:T(128)S(1)}, u32[]{:S(2)}) copy-start(s32[4]{0:T(128)S(1)} %reshape.250) | copy-start | bytes 52
  207.4 6.6 %copy-start.3 = (bf16[256,512]{1,0:T(8,128)(2,1)S(1)}, bf16[256,512]{1,0:T(8,128)(2,1)}, u32[]{:S(2)}) copy-start(bf16[256,512]{1,0:T(8,128)(2,1)} %get-tuple-element.262) | copy-start | bytes 786436
  207.4 6.6 %copy-start.7 = (bf16[256,512]{1,0:T(8,128)(2,1)S(1)}, bf16[256,512]{1,0:T(8,128)(2,1)}, u32[]{:S(2)}) copy-start(bf16[256,512]{1,0:T(8,128)(2,1)} %exchange_back.1) | copy-start | bytes 786436
  207.4 6.6 %copy-start.9 = (f32[1,256]{1,0:T(1,128)S(1)}, f32[1,256]{1,0:T(1,128)}, u32[]{:S(2)}) copy-start(f32[1,256]{1,0:T(1,128)} %param.23) | copy-start | bytes 3076
  207.4 6.6 %copy-start.11 = (f32[1,256]{1,0:T(1,128)S(1)}, f32[1,256]{1,0:T(1,128)}, u32[]{:S(2)}) copy-start(f32[1,256]{1,0:T(1,128)} %param.24) | copy-start | bytes 3076
  207.4 54.1 %all-to-all-start.2 = ((bf16[16,128,512]{2,1,0:T(8,128)(2,1)}), bf16[16,128,512]{2,1,0:T(8,128)(2,1)}, u32[]{:S(2)}, u32[]{:S(2)}) async-start(bf16[16,128,512]{2,1,0:T(8,128)(2,1)} %bitcast.79), calls=%async_computation.2 | async-start | bytes 4194304 | tf_op jit(solution)/shard_map/all_to_all | solution.py:549
  261.5 5.5 %copy-start.2 = (bf16[256,512]{1,0:T(8,128)(2,1)S(1)}, bf16[256,512]{1,0:T(8,128)(2,1)}, u32[]{:S(2)}) copy-start(bf16[256,512]{1,0:T(8,128)(2,1)} %get-tuple-element.268) | copy-start | bytes 786436
  261.5 52.5 %all-to-all-start.3 = ((bf16[16,128,512]{2,1,0:T(8,128)(2,1)}), bf16[16,128,512]{2,1,0:T(8,128)(2,1)S(1)}, u32[]{:S(2)}, u32[]{:S(2)}) async-start(bf16[16,128,512]{2,1,0:T(8,128)(2,1)} %bitcast.80), calls=%async_computation.3 | async-start | bytes 4194304 | tf_op jit(solution)/shard_map/all_to_all | solution.py:549
  267.1 0.9 copy-start.4
  267.1 1.0 copy-start.5
  267.1 1.1 copy-start.6
  313.9 1.3 copy-start.1
